TPU v7x, 32 devices: a whole 2x2x4 slice. The times are simulated.
32 devices in a mesh: rep: 4 (over z), fsdp: 2 (over x), ctx: 4 (over y, core).
Axes of the slice: x: 2, y: 2, z: 4, core: 2. Of those that a mesh axis runs over, the one named last changes fastest.
Arguments:
- tokens: bfloat16 [24, 1024, 768], P(('rep', 'fsdp'), 'ctx'), may hold values from -6 to 6
- segment: int32 [24, 1024], P(('rep', 'fsdp'), 'ctx'), may hold values from 0 to 3, never falling along the last dimension, each value on 1 to 512 neighbouring positions
- ln1_gain: bfloat16 [768], P(('fsdp', 'ctx')), may hold values from 0.099609375 to 1.8984375
- ln1_bias: bfloat16 [768], P(('fsdp', 'ctx')), may hold values from -1.75 to 1.75
- qkv_weight: bfloat16 [768, 2304], P(('fsdp', 'ctx')), may hold values from -0.21875 to 0.21875
- qkv_bias: bfloat16 [2304], P(('fsdp', 'ctx')), may hold values from -0.3125 to 0.3125
- out_weight: bfloat16 [768, 768], P(('fsdp', 'ctx')), may hold values from -1.75 to 1.75
- out_bias: bfloat16 [768], P(('fsdp', 'ctx')), may hold values from -1.75 to 1.75
- ln2_gain: bfloat16 [768], P(('fsdp', 'ctx')), may hold values from 0.099609375 to 1.8984375
- ln2_bias: bfloat16 [768], P(('fsdp', 'ctx')), may hold values from -1.75 to 1.75
- fc_weight: bfloat16 [768, 3072], P(('fsdp', 'ctx')), may hold values from -0.21875 to 0.21875
- fc_bias: bfloat16 [3072], P(('fsdp', 'ctx')), may hold values from -3 to 3
- proj_weight: bfloat16 [3072, 768], P(('fsdp', 'ctx')), may hold values from -0.109375 to 0.109375
- proj_bias: bfloat16 [768], P(('fsdp', 'ctx')), may hold values from -1.75 to 1.75
- cotangent: bfloat16 [24, 1024, 768], P(('rep', 'fsdp'), 'ctx'), may hold values from -6 to 6
Outputs:
- output: bfloat16 [24, 1024, 768], P(('rep', 'fsdp'), 'ctx')
- grad_tokens: bfloat16 [24, 1024, 768], P(('rep', 'fsdp'), 'ctx')
- grad_ln1_gain: float32 [768], P(('fsdp', 'ctx'))
- grad_ln1_bias: float32 [768], P(('fsdp', 'ctx'))
- grad_qkv_weight: float32 [768, 2304], P(('fsdp', 'ctx'))
- grad_qkv_bias: float32 [2304], P(('fsdp', 'ctx'))
- grad_out_weight: float32 [768, 768], P(('fsdp', 'ctx'))
- grad_out_bias: float32 [768], P(('fsdp', 'ctx'))
- grad_ln2_gain: float32 [768], P(('fsdp', 'ctx'))
- grad_ln2_bias: float32 [768], P(('fsdp', 'ctx'))
- grad_fc_weight: float32 [768, 3072], P(('fsdp', 'ctx'))
- grad_fc_bias: float32 [3072], P(('fsdp', 'ctx'))
- grad_proj_weight: float32 [3072, 768], P(('fsdp', 'ctx'))
- grad_proj_bias: float32 [768], P(('fsdp', 'ctx'))
All inputs are finite; a program needn't handle non-finite values.
Results may differ from a plain program's by a relative error of at most 0.017.
Values may be sent and summed in bfloat16 or wider, within the bound.
No kernel may reach another device: no remote copies, remote signals or barrier semaphores. Data moves between devices by JAX's collectives and lax.ppermute only.
A program may use at most 192 MiB of HBM per device.

v0:
```python
from functools import partial
import math

import jax
import jax.numpy as jnp
from jax import lax
from jax.sharding import PartitionSpec as P

HEADS = 12
HEAD = 64
ROT = 16


epsilon = 1e-05
far_below = -1e30
highest = lax.Precision.HIGHEST


def layer_norm(values, scales, shifts):
    center = values - jnp.mean(values, axis=-1, keepdims=True)
    spread = jnp.mean(center * center, axis=-1, keepdims=True)
    return center * lax.rsqrt(spread + epsilon) * scales + shifts


def exact_gelu(values):
    return jax.nn.gelu(values, approximate=False)


def wide_tables(places, features):
    inverse = 1.0 / 10000.0 ** (jnp.arange(0, ROT, 2).astype(jnp.float32) / ROT)
    column = jnp.arange(features, dtype=jnp.int32) % HEAD
    half_count = ROT // 2
    chosen = jnp.where(column < ROT, column % half_count, 0)
    picker = (chosen[:, None] == jnp.arange(half_count, dtype=jnp.int32)[None, :]).astype(
        jnp.float32
    )
    freq_row = jnp.sum(picker * inverse[None, :], axis=1)
    angles = places.astype(jnp.float32)[:, None] * freq_row[None, :]
    inside = (column < ROT)[None, :]
    cosine_table = jnp.where(inside, jnp.cos(angles), 1.0)
    sine_table = jnp.where(inside, jnp.sin(angles), 0.0)
    return (cosine_table, sine_table)


def swap_matrix(features):
    source = jnp.arange(features, dtype=jnp.int32)
    target = jnp.arange(features, dtype=jnp.int32)
    local_tgt = target % HEAD
    half_count = ROT // 2
    from_upper = (local_tgt < half_count)[None, :] & (
        source[:, None] == target[None, :] + half_count
    )
    from_lower = ((local_tgt >= half_count) & (local_tgt < ROT))[None, :] & (
        source[:, None] == target[None, :] - half_count
    )
    return jnp.where(from_upper, -1.0, 0.0) + jnp.where(from_lower, 1.0, 0.0)


def rotate_wide(rows_in, cosine_table, sine_table, swapper):
    swapped = jnp.dot(rows_in, swapper, precision=highest)
    return rows_in * cosine_table + swapped * sine_table


def to_heads(seq_rows):
    seq_count, rows_in, features = seq_rows.shape
    return seq_rows.reshape(seq_count, rows_in, HEADS, HEAD).transpose(0, 2, 1, 3)


def from_heads(head_rows):
    seq_count, heads_in, rows_in, size_in = head_rows.shape
    return head_rows.transpose(0, 2, 1, 3).reshape(seq_count, rows_in, heads_in * size_in)


def trans_left(matrix_a, matrix_b):
    return lax.dot_general(
        matrix_a, matrix_b, (((0,), (0,)), ((), ())), preferred_element_type=jnp.float32
    )


def trans_right(matrix_a, matrix_b):
    return lax.dot_general(
        matrix_a, matrix_b, (((1,), (1,)), ((), ())), preferred_element_type=jnp.float32
    )


def block_scores(query_part, key_part, query_seg, key_seg, query_place, key_place):
    scaled = jnp.einsum(
        "phqd,phkd->phqk", query_part, key_part, preferred_element_type=jnp.float32
    ) * (1.0 / math.sqrt(HEAD))
    allowed = (query_seg[:, None, :, None] == key_seg[:, None, None, :]) & (
        key_place[None, None, None, :] <= query_place[None, None, :, None]
    )
    return (scaled, allowed)


def attend_block(block_in, query_place, key_place):
    query_part, key_part, value_part, query_seg, key_seg = block_in
    scaled, allowed = block_scores(query_part, key_part, query_seg, key_seg, query_place, key_place)
    masked = jnp.where(allowed, scaled, far_below)
    row_max = jnp.max(masked, axis=-1, keepdims=True)
    lifted = jnp.exp(masked - row_max)
    row_sum = jnp.sum(lifted, axis=-1, keepdims=True)
    weights = (lifted / row_sum).astype(jnp.bfloat16)
    combined = jnp.einsum(
        "phqk,phkd->phqd", weights, value_part, preferred_element_type=jnp.float32
    )
    return (combined.astype(jnp.bfloat16), (row_max + jnp.log(row_sum))[..., 0])


def score_grads(block_in, query_place, key_place, row_inner):
    query_part, key_part, value_part, query_seg, key_seg, grad_combined, log_sums = block_in
    scaled, allowed = block_scores(query_part, key_part, query_seg, key_seg, query_place, key_place)
    weights = jnp.where(allowed, jnp.exp(scaled - log_sums[..., None]), 0.0)
    grad_weights = jnp.einsum(
        "phqd,phkd->phqk", grad_combined, value_part, preferred_element_type=jnp.float32
    )
    row_inner = jnp.sum(weights * grad_weights, axis=-1)
    grad_scores = (weights * (grad_weights - row_inner[..., None])).astype(jnp.bfloat16)
    return (weights, grad_scores, row_inner)


def return_block(block_in, query_place, key_place):
    query_part, key_part, value_part, query_seg, key_seg, grad_combined, log_sums = block_in
    weights, grad_scores, row_inner = score_grads(block_in, query_place, key_place, None)
    factor = 1.0 / math.sqrt(HEAD)
    grad_query = (
        jnp.einsum("phqk,phkd->phqd", grad_scores, key_part, preferred_element_type=jnp.float32)
        * factor
    )
    grad_key = (
        jnp.einsum("phqk,phqd->phkd", grad_scores, query_part, preferred_element_type=jnp.float32)
        * factor
    )
    grad_value = jnp.einsum(
        "phqk,phqd->phkd",
        weights.astype(jnp.bfloat16),
        grad_combined,
        preferred_element_type=jnp.float32,
    )
    return (grad_query, grad_key, grad_value)


def shards(
    tokens,
    segment,
    ln1_gain,
    ln1_bias,
    qkv_weight,
    qkv_bias,
    out_weight,
    out_bias,
    ln2_gain,
    ln2_bias,
    fc_weight,
    fc_bias,
    proj_weight,
    proj_bias,
    cotangent,
):
    gathered = (
        lax.all_gather(ln1_gain, ("fsdp", "ctx"), axis=0, tiled=True),
        lax.all_gather(ln1_bias, ("fsdp", "ctx"), axis=0, tiled=True),
        lax.all_gather(qkv_weight, ("fsdp", "ctx"), axis=0, tiled=True),
        lax.all_gather(qkv_bias, ("fsdp", "ctx"), axis=0, tiled=True),
        lax.all_gather(out_weight, ("fsdp", "ctx"), axis=0, tiled=True),
        lax.all_gather(out_bias, ("fsdp", "ctx"), axis=0, tiled=True),
        lax.all_gather(ln2_gain, ("fsdp", "ctx"), axis=0, tiled=True),
        lax.all_gather(ln2_bias, ("fsdp", "ctx"), axis=0, tiled=True),
        lax.all_gather(fc_weight, ("fsdp", "ctx"), axis=0, tiled=True),
        lax.all_gather(fc_bias, ("fsdp", "ctx"), axis=0, tiled=True),
        lax.all_gather(proj_weight, ("fsdp", "ctx"), axis=0, tiled=True),
        lax.all_gather(proj_bias, ("fsdp", "ctx"), axis=0, tiled=True),
    )
    (
        gain_one,
        shift_one,
        w_qkv,
        b_qkv,
        w_out,
        b_out,
        gain_two,
        shift_two,
        w_fc,
        b_fc,
        w_proj,
        b_proj,
    ) = gathered
    seq_count, local_len, features = tokens.shape
    length = local_len * lax.axis_size("ctx")
    total_rows = seq_count * local_len
    flat_rows = tokens.reshape(total_rows, features).astype(jnp.float32)
    norm_one, back_one = jax.vjp(
        layer_norm, flat_rows, gain_one.astype(jnp.float32), shift_one.astype(jnp.float32)
    )
    first_in = norm_one.astype(jnp.bfloat16)
    qkv_rows = jnp.dot(first_in, w_qkv, preferred_element_type=jnp.float32) + b_qkv.astype(
        jnp.float32
    )
    query_place = lax.axis_index("ctx") * local_len + jnp.arange(local_len, dtype=jnp.int32)
    full_place = jnp.arange(length, dtype=jnp.int32)
    cosine_table, sine_table = wide_tables(jnp.tile(query_place, seq_count), features)
    swapper = swap_matrix(features)
    query_part = rotate_wide(qkv_rows[:, :features], cosine_table, sine_table, swapper).astype(
        jnp.bfloat16
    )
    key_part = rotate_wide(
        qkv_rows[:, features : 2 * features], cosine_table, sine_table, swapper
    ).astype(jnp.bfloat16)
    value_part = qkv_rows[:, 2 * features :].astype(jnp.bfloat16)
    query_seq = query_part.reshape(seq_count, local_len, features)
    key_seq = key_part.reshape(seq_count, local_len, features)
    value_seq = value_part.reshape(seq_count, local_len, features)
    seg_wire = segment.astype(jnp.bfloat16)
    all_keys, all_values, all_segs = (
        lax.all_gather(key_seq, "ctx", axis=1, tiled=True),
        lax.all_gather(value_seq, "ctx", axis=1, tiled=True),
        lax.all_gather(seg_wire, "ctx", axis=1, tiled=True),
    )
    per_block = max(1, min(seq_count, 512 // local_len))
    while seq_count % per_block:
        per_block -= 1
    blocks = seq_count // per_block
    query_tiles = to_heads(query_seq).reshape(blocks, per_block, HEADS, local_len, HEAD)
    query_segs = segment.astype(jnp.float32).reshape(blocks, per_block, local_len)
    rows_in = all_keys.shape[1]
    key_tiles = to_heads(all_keys).reshape(blocks, per_block, HEADS, rows_in, HEAD)
    value_tiles = to_heads(all_values).reshape(blocks, per_block, HEADS, rows_in, HEAD)
    key_segs = all_segs.astype(jnp.float32).reshape(blocks, per_block, rows_in)
    attended_tiles, log_sums = lax.map(
        partial(attend_block, query_place=query_place, key_place=full_place),
        (query_tiles, key_tiles, value_tiles, query_segs, key_segs),
    )
    attended = from_heads(attended_tiles.reshape(seq_count, HEADS, local_len, HEAD)).reshape(
        total_rows, features
    )
    branch = jnp.dot(attended, w_out, preferred_element_type=jnp.float32) + b_out.astype(
        jnp.float32
    )
    norm_two, back_two = jax.vjp(
        layer_norm, flat_rows, gain_two.astype(jnp.float32), shift_two.astype(jnp.float32)
    )
    second_in = norm_two.astype(jnp.bfloat16)
    before = jnp.dot(second_in, w_fc, preferred_element_type=jnp.float32) + b_fc.astype(jnp.float32)
    active, back_gelu = jax.vjp(exact_gelu, before)
    hidden = active.astype(jnp.bfloat16)
    summed = (
        flat_rows
        + branch
        + jnp.dot(hidden, w_proj, preferred_element_type=jnp.float32)
        + b_proj.astype(jnp.float32)
    )
    output = summed.astype(jnp.bfloat16).reshape(tokens.shape)
    w_qkv_back, w_out_back, w_fc_back, w_proj_back = (
        lax.all_gather(qkv_weight, ("fsdp", "ctx"), axis=0, tiled=True),
        lax.all_gather(out_weight, ("fsdp", "ctx"), axis=0, tiled=True),
        lax.all_gather(fc_weight, ("fsdp", "ctx"), axis=0, tiled=True),
        lax.all_gather(proj_weight, ("fsdp", "ctx"), axis=0, tiled=True),
    )
    grad_rows = cotangent.reshape(total_rows, features)
    grad_attended = trans_right(grad_rows, w_out_back).astype(jnp.bfloat16)
    grad_w_out = trans_left(attended, grad_rows)
    grad_b_out = jnp.sum(grad_rows.astype(jnp.float32), axis=0)
    grad_hidden = trans_right(grad_rows, w_proj_back)
    grad_w_proj = trans_left(hidden, grad_rows)
    grad_before = back_gelu(grad_hidden)[0].astype(jnp.bfloat16)
    grad_w_fc = trans_left(second_in, grad_before)
    grad_b_fc = jnp.sum(grad_before.astype(jnp.float32), axis=0)
    grad_second = trans_right(grad_before, w_fc_back)
    grad_flat_two, grad_gain_two, grad_shift_two = back_two(grad_second)
    back_keys, back_values, back_segs = (key_tiles, value_tiles, key_segs)
    grad_att_seq = grad_attended.reshape(seq_count, local_len, features)
    grad_att_tiles = to_heads(grad_att_seq).reshape(blocks, per_block, HEADS, local_len, HEAD)
    grad_query_tiles, grad_key_tiles, grad_value_tiles = lax.map(
        partial(return_block, query_place=query_place, key_place=full_place),
        (query_tiles, back_keys, back_values, query_segs, back_segs, grad_att_tiles, log_sums),
    )
    key_full = from_heads(grad_key_tiles.reshape(seq_count, HEADS, length, HEAD))
    value_full = from_heads(grad_value_tiles.reshape(seq_count, HEADS, length, HEAD))
    key_sums, value_sums = (
        lax.psum_scatter(
            key_full.astype(jnp.bfloat16), "ctx", scatter_dimension=1, tiled=True
        ).astype(jnp.float32),
        lax.psum_scatter(
            value_full.astype(jnp.bfloat16), "ctx", scatter_dimension=1, tiled=True
        ).astype(jnp.float32),
    )
    query_grad_rows = from_heads(
        grad_query_tiles.reshape(seq_count, HEADS, local_len, HEAD)
    ).reshape(total_rows, features)
    grad_query = rotate_wide(query_grad_rows, cosine_table, -sine_table, swapper)
    grad_key = rotate_wide(
        key_sums.reshape(total_rows, features), cosine_table, -sine_table, swapper
    )
    grad_qkv = jnp.concatenate(
        [grad_query, grad_key, value_sums.reshape(total_rows, features)], axis=1
    ).astype(jnp.bfloat16)
    grad_w_qkv = trans_left(first_in, grad_qkv)
    grad_b_qkv = jnp.sum(grad_qkv.astype(jnp.float32), axis=0)
    grad_first = trans_right(grad_qkv, w_qkv_back)
    grad_flat_one, grad_gain_one, grad_shift_one = back_one(grad_first)
    grad_tokens = (
        (grad_rows.astype(jnp.float32) + grad_flat_one + grad_flat_two)
        .astype(jnp.bfloat16)
        .reshape(tokens.shape)
    )
    owned = (
        lax.psum_scatter(
            grad_gain_one.astype(jnp.bfloat16), ("fsdp", "ctx"), scatter_dimension=0, tiled=True
        ).astype(jnp.float32),
        lax.psum_scatter(
            grad_shift_one.astype(jnp.bfloat16), ("fsdp", "ctx"), scatter_dimension=0, tiled=True
        ).astype(jnp.float32),
        lax.psum_scatter(
            grad_w_qkv.astype(jnp.bfloat16), ("fsdp", "ctx"), scatter_dimension=0, tiled=True
        ).astype(jnp.float32),
        lax.psum_scatter(
            grad_b_qkv.astype(jnp.bfloat16), ("fsdp", "ctx"), scatter_dimension=0, tiled=True
        ).astype(jnp.float32),
        lax.psum_scatter(
            grad_w_out.astype(jnp.bfloat16), ("fsdp", "ctx"), scatter_dimension=0, tiled=True
        ).astype(jnp.float32),
        lax.psum_scatter(
            grad_b_out.astype(jnp.bfloat16), ("fsdp", "ctx"), scatter_dimension=0, tiled=True
        ).astype(jnp.float32),
        lax.psum_scatter(
            grad_gain_two.astype(jnp.bfloat16), ("fsdp", "ctx"), scatter_dimension=0, tiled=True
        ).astype(jnp.float32),
        lax.psum_scatter(
            grad_shift_two.astype(jnp.bfloat16), ("fsdp", "ctx"), scatter_dimension=0, tiled=True
        ).astype(jnp.float32),
        lax.psum_scatter(
            grad_w_fc.astype(jnp.bfloat16), ("fsdp", "ctx"), scatter_dimension=0, tiled=True
        ).astype(jnp.float32),
        lax.psum_scatter(
            grad_b_fc.astype(jnp.bfloat16), ("fsdp", "ctx"), scatter_dimension=0, tiled=True
        ).astype(jnp.float32),
        lax.psum_scatter(
            grad_w_proj.astype(jnp.bfloat16), ("fsdp", "ctx"), scatter_dimension=0, tiled=True
        ).astype(jnp.float32),
        lax.psum_scatter(
            grad_b_out.astype(jnp.bfloat16), ("fsdp", "ctx"), scatter_dimension=0, tiled=True
        ).astype(jnp.float32),
    )
    (
        own_gain_one,
        own_shift_one,
        own_w_qkv,
        own_b_qkv,
        own_w_out,
        own_b_out,
        own_gain_two,
        own_shift_two,
        own_w_fc,
        own_b_fc,
        own_w_proj,
        own_b_proj,
    ) = owned
    finished = (
        lax.psum(own_gain_one.astype(jnp.bfloat16), "rep").astype(jnp.float32),
        lax.psum(own_shift_one.astype(jnp.bfloat16), "rep").astype(jnp.float32),
        lax.psum(own_w_qkv.astype(jnp.bfloat16), "rep").astype(jnp.float32),
        lax.psum(own_b_qkv.astype(jnp.bfloat16), "rep").astype(jnp.float32),
        lax.psum(own_w_out.astype(jnp.bfloat16), "rep").astype(jnp.float32),
        lax.psum(own_b_out.astype(jnp.bfloat16), "rep").astype(jnp.float32),
        lax.psum(own_gain_two.astype(jnp.bfloat16), "rep").astype(jnp.float32),
        lax.psum(own_shift_two.astype(jnp.bfloat16), "rep").astype(jnp.float32),
        lax.psum(own_w_fc.astype(jnp.bfloat16), "rep").astype(jnp.float32),
        lax.psum(own_b_fc.astype(jnp.bfloat16), "rep").astype(jnp.float32),
        lax.psum(own_w_proj.astype(jnp.bfloat16), "rep").astype(jnp.float32),
        lax.psum(own_b_proj.astype(jnp.bfloat16), "rep").astype(jnp.float32),
    )
    return (
        output,
        grad_tokens,
        finished[0],
        finished[1],
        finished[2],
        finished[3],
        finished[4],
        finished[5],
        finished[6],
        finished[7],
        finished[8],
        finished[9],
        finished[10],
        finished[11],
    )


def solution(mesh):
    in_specs = (
        P(("rep", "fsdp"), "ctx", None),
        P(("rep", "fsdp"), "ctx"),
        P(("fsdp", "ctx")),
        P(("fsdp", "ctx")),
        P(("fsdp", "ctx"), None),
        P(("fsdp", "ctx")),
        P(("fsdp", "ctx"), None),
        P(("fsdp", "ctx")),
        P(("fsdp", "ctx")),
        P(("fsdp", "ctx")),
        P(("fsdp", "ctx"), None),
        P(("fsdp", "ctx")),
        P(("fsdp", "ctx"), None),
        P(("fsdp", "ctx")),
        P(("rep", "fsdp"), "ctx", None),
    )
    out_specs = (
        P(("rep", "fsdp"), "ctx", None),
        P(("rep", "fsdp"), "ctx", None),
        P(("fsdp", "ctx")),
        P(("fsdp", "ctx")),
        P(("fsdp", "ctx"), None),
        P(("fsdp", "ctx")),
        P(("fsdp", "ctx"), None),
        P(("fsdp", "ctx")),
        P(("fsdp", "ctx")),
        P(("fsdp", "ctx")),
        P(("fsdp", "ctx"), None),
        P(("fsdp", "ctx")),
        P(("fsdp", "ctx"), None),
        P(("fsdp", "ctx")),
    )
    return jax.shard_map(shards, mesh=mesh, in_specs=in_specs, out_specs=out_specs, check_vma=False)
```

profile of v0, /device:TPU:0, one launch (start us, length us, event | category | flops | bytes accessed | tf_op | source)
XLA Modules:
  0.0 698.7 jit_solution(3933052919042707681)
XLA Ops:
  14.0 26.0 %all-reduce.15 = (bf16[768]{0:T(1024)(128)(2,1)S(1)}, bf16[768]{0:T(1024)(128)(2,1)S(1)}, bf16[768]{0:T(1024)(128)(2,1)S(1)}, bf16[768]{0:T(1024)(128)(2,1)S(1)}, bf16[2304]{0:T(1024)(128)(2,1)S(1)}) all-reduce(bf16[768]{0:T(1024)(128)(2,1)S(1)} %dynamic-update-slice.5, ...), channel_id=1, replica_groups=mesh['rep'=4,'fsdp'=2,'ctx'=4] {'fsdp','ctx'}, use_global_device_ids=true, to_apply=%add.5 | all-reduce | flops 5376 | bytes 21504
  42.5 4.4 all-gather.8.cloned.1.call-done
  46.9 4.9 convolution_add_fusion
  52.0 16.3 %fusion.86 = bf16[768,768]{1,0:T(8,128)(2,1)} fusion(f32[768,2304]{1,0:T(8,128)S(1)} %convolution_add_fusion, s32[768]{0:T(1024)S(1)} %get-tuple-element.349, s32[768]{0:T(1024)S(1)} %get-tuple-element.350, f32[768]{0:T(1024)S(1)} %select_reduce_fusion, f32[768]{0:T(1024)S(1)} %convert_element_type.233, pred[768]{0:T(1024)(128)(4,1)S(1)} %fusion.174, ...), kind=kOutput, calls=%fused_computation.107 | convolution fusion | flops 5444075520 | bytes 5917696 | tf_op jit(solution)/shard_map/dot_general | solution.py:60
  72.6 5.2 all_gather.49
  85.3 17.8 %fusion.84 = bf16[768,768]{1,0:T(8,128)(2,1)S(1)} fusion(f32[768,2304]{1,0:T(8,128)} %copy-done.22, s32[768]{0:T(1024)S(1)} %copy-done.42, s32[768]{0:T(1024)S(1)} %copy-done.45, f32[768]{0:T(1024)S(1)} %copy-done.48, f32[768]{0:T(1024)S(1)} %copy-done.39, pred[768]{0:T(1024)(128)(4,1)S(1)} %copy-done.65, pred[768]{0:T(1024)(128)(4,1)S(1)} %copy-done.54, ...), kind=kOutput, calls=%fused_computation.105 | convolution fusion | flops 5444075520 | bytes 5912832 | tf_op jit(solution)/shard_map/dot_general | solution.py:60
  107.3 5.2 all-gather.10.cloned.1.call-done
  112.5 6.6 copy.67
  119.2 32.8 %all-gather.12.cloned.1.call-done = bf16[3,1024,768]{2,1,0:T(8,128)(2,1)} async-done(((bf16[3,256,768]{2,1,0:T(8,128)(2,1)}), bf16[3,1024,768]{2,1,0:T(8,128)(2,1)}) %all-gather.12.cloned.1.call-update) | async-done | bytes 4718608 | tf_op jit(solution)/shard_map/all_gather | solution.py:216
  152.0 6.6 copy.68
  158.7 40.7 %while.28 = (s32[]{:T(128)}, bf16[3,1,12,256,64]{3,4,2,1,0:T(8,128)(2,1)S(1)}, f32[3,1,12,256]{3,2,1,0:T(8,128)}, f32[3,1,256]{2,1,0:T(1,128)S(1)}, f32[3,1,1024...) while((s32[]{:T(128)}, ...), condition=%wide.region_6.7_spmd.clone, body=%wide.region_3.6_spmd.clone.sunk | while | flops 844035328 | bytes 42860144 | solution.py:229
  167.3 5.1 fusion.247
  180.8 5.1 fusion.247
  194.3 5.1 fusion.247
  200.4 92.1 %while.29 = (s32[]{:T(128)}, f32[3,1,12,256,64]{3,4,2,1,0:T(8,128)}, bf16[3,1,12,1024,64]{3,4,2,1,0:T(8,128)(2,1)}, bf16[3,1,12,1024,64]{3,4,2,1,0:T(8,128)(2,1)...) while((s32[]{:T(128)}, ...), condition=%wide.region_9.10_spmd.clone, body=%wide.region_7.9_spmd.clone.sunk | while | flops 2062218496 | bytes 108906640 | solution.py:273
  204.9 8.8 %multiply_reduce_fusion.2 = (f32[12,256]{1,0:T(8,128)S(1)}, f32[12,256,1024]{2,1,0:T(8,128)}) fusion(f32[12,256,1024]{2,1,0:T(8,128)S(1)} %fusion.256, f32[12,256]{1,0:T(8,128)S(1)} %dynamic-slice_bitcast_fusion.2, pred[256,1024]{1,0:T(8,128)(4,1)S(1)} %fusion.257, bf16[3,1,12,1024,64]{3,4,2,1,0:T(8,128)(2,1)} %get-tuple-element.555, ...), kind=kOutput, calls=%fused_computation.31.clone.1 | convolution fusion | flops 418378752 | bytes 27423744 | tf_op jit(solution)/shard_map/while/body/eval_jaxpr/phqd,phkd->phqk/dot_general | solution.py:114
  213.7 6.7 multiply_convert_fusion.3
  222.9 4.4 fusion.258
  235.6 8.8 %multiply_reduce_fusion.2 = (f32[12,256]{1,0:T(8,128)S(1)}, f32[12,256,1024]{2,1,0:T(8,128)}) fusion(f32[12,256,1024]{2,1,0:T(8,128)S(1)} %fusion.256, f32[12,256]{1,0:T(8,128)S(1)} %dynamic-slice_bitcast_fusion.2, pred[256,1024]{1,0:T(8,128)(4,1)S(1)} %fusion.257, bf16[3,1,12,1024,64]{3,4,2,1,0:T(8,128)(2,1)} %get-tuple-element.555, ...), kind=kOutput, calls=%fused_computation.31.clone.1 | convolution fusion | flops 418378752 | bytes 27423744 | tf_op jit(solution)/shard_map/while/body/eval_jaxpr/phqd,phkd->phqk/dot_general | solution.py:114
  244.4 6.7 multiply_convert_fusion.3
  253.5 4.3 fusion.258
  257.8 4.0 bitcast_dynamic-update-slice_fusion.8
  266.2 8.8 %multiply_reduce_fusion.2 = (f32[12,256]{1,0:T(8,128)S(1)}, f32[12,256,1024]{2,1,0:T(8,128)}) fusion(f32[12,256,1024]{2,1,0:T(8,128)S(1)} %fusion.256, f32[12,256]{1,0:T(8,128)S(1)} %dynamic-slice_bitcast_fusion.2, pred[256,1024]{1,0:T(8,128)(4,1)S(1)} %fusion.257, bf16[3,1,12,1024,64]{3,4,2,1,0:T(8,128)(2,1)} %get-tuple-element.555, ...), kind=kOutput, calls=%fused_computation.31.clone.1 | convolution fusion | flops 418378752 | bytes 27423744 | tf_op jit(solution)/shard_map/while/body/eval_jaxpr/phqd,phkd->phqk/dot_general | solution.py:114
  275.0 6.7 multiply_convert_fusion.3
  284.1 4.3 fusion.258
  288.4 4.0 bitcast_dynamic-update-slice_fusion.8
  292.5 6.7 copy.77
  299.2 6.7 copy.79
  306.6 9.1 %all-gather = bf16[8,1,384]{2,1,0:T(2,128)(2,1)S(1)} all-gather(bf16[1,1,384]{2,1,0:T(2,128)(2,1)S(1)} %reshape.546), channel_id=1, replica_groups=mesh['rep'=4,'fsdp'=2,'ctx'=4] {'fsdp','ctx'}, dimensions={0}, use_global_device_ids=true | all-gather | bytes 6912 | tf_op jit(solution)/shard_map/all_gather | solution.py:170
  315.7 9.0 %fusion.198 = f32[768,3072]{1,0:T(8,128)} fusion(bf16[768,768]{1,0:T(8,128)(2,1)S(1)} %copy-done.9, bf16[768,3072]{1,0:T(8,128)(2,1)} %all-gather.16.cloned.1.call-done), kind=kOutput, calls=%fused_computation.233 | convolution fusion | flops 3623878656 | bytes 15335424 | tf_op jit(solution)/shard_map/dot_general | solution.py:243
  324.7 29.5 %fusion.194 = (bf16[3072]{0:T(1024)(128)(2,1)}, bf16[768,3072]{1,0:T(8,128)(2,1)}, f32[768,3072]{1,0:T(8,128)}) fusion(f32[768,3072]{1,0:T(8,128)} %fusion.198, f32[3072]{0:T(1024)S(1)} %bitcast.278, bf16[768,768]{1,0:T(8,128)(2,1)S(1)} %bitcast.262, bf16[3072,768]{1,0:T(8,128)(2,1)} %all-gather.18.cloned.1.call-done), kind=kOutput, calls=%fused_computation.230 | convolution fusion | flops 3798463488 | bytes 29509632 | tf_op jit(solution)/shard_map/dot_general | solution.py:81
  357.7 12.4 %multiply_convert_fusion.1 = bf16[768,3072]{1,0:T(8,128)(2,1)} fusion(f32[768,3072]{1,0:T(8,128)} %get-tuple-element.333, f32[768,3072]{1,0:T(8,128)} %fusion.198, f32[3072]{0:T(1024)S(1)} %bitcast.279), kind=kLoop, calls=%fused_computation.74 | loop fusion | flops 9437184 | bytes 23605248 | tf_op jit(solution)/shard_map/convert_element_type | solution.py:245
  370.1 8.0 %convolution_convert_fusion.1 = bf16[3072,768]{1,0:T(8,128)(2,1)} fusion(bf16[768,3072]{1,0:T(8,128)(2,1)} %multiply_convert_fusion.1, bf16[768,768]{1,0:T(8,128)(2,1)S(1)} %bitcast.264), kind=kOutput, calls=%fused_computation.90 | convolution fusion | flops 3626237952 | bytes 10616832 | tf_op jit(solution)/shard_map/dot_general | solution.py:75
  378.2 8.2 %convolution_convert_fusion.2 = bf16[768,3072]{1,0:T(8,128)(2,1)} fusion(bf16[768,768]{1,0:T(8,128)(2,1)S(1)} %copy-done.9, bf16[768,3072]{1,0:T(8,128)(2,1)} %get-tuple-element.332), kind=kOutput, calls=%fused_computation.91 | convolution fusion | flops 3626237952 | bytes 10616832 | tf_op jit(solution)/shard_map/dot_general | solution.py:75
  392.3 19.3 %fusion.88 = bf16[768,768]{1,0:T(8,128)(2,1)} fusion(f32[768,768]{1,0:T(8,128)} %copy.75, f32[768,768]{0,1:T(8,128)S(1)} %bitcast.254, s32[768]{0:T(1024)S(1)} %copy-done.43, s32[768]{0:T(1024)S(1)} %copy-done.46, f32[768]{0:T(1024)S(1)} %copy-done.49, f32[768]{0:T(1024)S(1)} %copy-done.40, pred[768]{0:T(1024)(128)(4,1)} %copy-done.64, ...), kind=kOutput, calls=%fused_computation.109 | convolution fusion | flops 5444665344 | bytes 5912832 | tf_op jit(solution)/shard_map/dot_general | solution.py:60
  411.6 16.4 %fusion.90 = bf16[768,768]{1,0:T(8,128)(2,1)} fusion(bf16[768,768]{1,0:T(8,128)(2,1)} %bitcast.280, s32[768]{0:T(1024)S(1)} %copy-done.43, s32[768]{0:T(1024)S(1)} %copy-done.46, f32[768]{0:T(1024)S(1)} %copy-done.49, f32[768]{0:T(1024)S(1)} %copy-done.40, pred[768]{0:T(1024)(128)(4,1)} %copy-done.64, pred[768]{0:T(1024)(128)(4,1)} %copy-done.53, ...), kind=kOutput, calls=%fused_computation.111 | convolution fusion | flops 5445255168 | bytes 2373888 | tf_op jit(solution)/shard_map/dot_general | solution.py:60
  428.1 6.4 convolution_convert_fusion
  440.3 7.1 %fusion.200 = f32[768,768]{1,0:T(8,128)S(1)} fusion(bf16[768,3072]{1,0:T(8,128)(2,1)} %get-tuple-element.332, bf16[768,3072]{1,0:T(8,128)(2,1)} %all-gather.16.cloned.1.call-done), kind=kOutput, calls=%fused_computation.235 | convolution fusion | flops 3623878656 | bytes 11796480 | tf_op jit(solution)/shard_map/dot_general | solution.py:81
  447.5 9.9 %fusion.199 = f32[768,768]{1,0:T(8,128)} fusion(bf16[768,3072]{1,0:T(8,128)(2,1)} %multiply_convert_fusion.1, bf16[3072,768]{1,0:T(8,128)(2,1)} %all-gather.18.cloned.1.call-done), kind=kOutput, calls=%fused_computation.234 | convolution fusion | flops 3623878656 | bytes 11796480 | tf_op jit(solution)/shard_map/dot_general | solution.py:249
  457.5 5.3 fusion.193
  463.4 32.9 %reduce-scatter.17.cloned.1.call-done = bf16[384,768]{1,0:T(8,128)(2,1)} async-done(((bf16[3072,768]{1,0:T(8,128)(2,1)}), bf16[384,768]{1,0:T(8,128)(2,1)}) %reduce-scatter.17.cloned.1.call-update) | async-done | bytes 589840 | tf_op jit(solution)/shard_map/reduce_scatter | solution.py:337
  496.3 57.4 %reduce-scatter.15.cloned.1.call-done = bf16[96,3072]{1,0:T(8,128)(2,1)} async-done(((bf16[768,3072]{1,0:T(8,128)(2,1)}), bf16[96,3072]{1,0:T(8,128)(2,1)}) %reduce-scatter.15.cloned.1.call-update) | async-done | bytes 589840 | tf_op jit(solution)/shard_map/reduce_scatter | solution.py:331
  553.7 51.8 %reduce-scatter.11.cloned.1.call-done = bf16[96,2304]{1,0:T(8,128)(2,1)} async-done(((bf16[768,2304]{1,0:T(8,128)(2,1)}), bf16[96,2304]{1,0:T(8,128)(2,1)}) %reduce-scatter.11.cloned.1.call-update) | async-done | bytes 442384 | tf_op jit(solution)/shard_map/reduce_scatter | solution.py:313
  605.6 4.5 fusion.111
  611.3 25.6 %all-reduce.14 = (bf16[768]{0:T(1024)(128)(2,1)}, bf16[768]{0:T(1024)(128)(2,1)}, bf16[768]{0:T(1024)(128)(2,1)}, bf16[768]{0:T(1024)(128)(2,1)}, bf16[2304]{0:T...) all-reduce(bf16[768]{0:T(1024)(128)(2,1)} %copy-done.36, ...), channel_id=1, replica_groups=mesh['rep'=4,'fsdp'=2,'ctx'=4] {'fsdp','ctx'}, use_global_device_ids=true, to_apply=%add.6 | all-reduce | flops 10752 | bytes 43008
  645.8 13.1 %all-reduce.16 = (bf16[96]{0:T(256)(128)(2,1)}, bf16[96]{0:T(256)(128)(2,1)}, bf16[288]{0:T(512)(128)(2,1)}, bf16[96]{0:T(256)(128)(2,1)}, bf16[96]{0:T(256)(128...) all-reduce(bf16[96]{0:T(256)(128)(2,1)} %dynamic-slice.8, ...), channel_id=1, replica_groups=mesh['rep'=4,'fsdp'=2,'ctx'=4] {'rep'}, use_global_device_ids=true, to_apply=%region_18.19 | all-reduce | flops 1152 | bytes 4608 | tf_op jit(solution)/shard_map/psum | solution.py:359
  670.0 4.8 fusion.118
  677.6 7.5 %all-reduce.20.cloned.1.call-done = (bf16[96,2304]{1,0:T(8,128)(2,1)}, bf16[96,768]{1,0:T(8,128)(2,1)}, bf16[96,3072]{1,0:T(8,128)(2,1)}, bf16[384,768]{1,0:T(8,128)(2,1)}) async-done(((bf16[96,2304]{1,0:T(8,128)(2,1)}, bf16[96,768]{1,0:T(8,128)(2,1)}, bf16[96,3072]{1,0:T(8,128)(2,1)}, bf16[384,768]{1,0:T(8,128)(2,1)}), (bf16[96,2304]{1,0:T(8,128)(2,1)}, bf16[96,768]{1,0:T(8,128)(2,1)}, ...) | async-done | bytes 1769488 | tf_op jit(solution)/shard_map/psum | solution.py:361
  (297 shorter events, 119.3 us)
Async XLA Ops:
  7.2 5.6 copy-start.58
  7.2 5.8 copy-start.59
  7.2 6.1 copy-start.60
  7.2 6.3 copy-start.61
  7.2 6.5 copy-start.51
  7.3 39.7 %all-gather.8.cloned.1.call-start = ((), (), s32[]{:S(2)}) async-start(), calls=%async_computation.6 | async-start | bytes 3981312 | tf_op jit(solution)/shard_map/all_gather | solution.py:163
  8.0 69.8 %all-gather.14.cloned.1.call-start = ((), (), s32[]{:S(2)}) async-start(), calls=%async_computation.9 | async-start | bytes 1327104 | tf_op jit(solution)/shard_map/all_gather | solution.py:165
  8.7 103.8 %all-gather.10.cloned.1.call-start = ((), (), s32[]{:S(2)}) async-start(), calls=%async_computation.7 | async-start | bytes 5898240 | tf_op jit(solution)/shard_map/all_gather | solution.py:215
  8.8 43.1 %copy-start.64 = (pred[768]{0:T(1024)(128)(4,1)}, pred[768]{0:T(1024)(128)(4,1)S(1)}, u32[]{:S(2)}) copy-start(pred[768]{0:T(1024)(128)(4,1)S(1)} %fusion.174) | copy-start | bytes 2308
  10.9 41.0 %copy-start.24 = (f32[768]{0:T(1024)}, f32[768]{0:T(1024)S(1)}, u32[]{:S(2)}) copy-start(f32[768]{0:T(1024)S(1)} %div.45) | copy-start | bytes 9220
  40.1 11.8 %copy-start.26 = (f32[768]{0:T(1024)}, f32[768]{0:T(1024)S(1)}, u32[]{:S(2)}) copy-start(f32[768]{0:T(1024)S(1)} %convert_element_type.228) | copy-start | bytes 9220
  40.1 11.8 %copy-start.28 = (f32[768]{0:T(1024)}, f32[768]{0:T(1024)S(1)}, u32[]{:S(2)}) copy-start(f32[768]{0:T(1024)S(1)} %convert_element_type.238) | copy-start | bytes 9220
  40.2 11.7 %copy-start.30 = (f32[768]{0:T(1024)}, f32[768]{0:T(1024)S(1)}, u32[]{:S(2)}) copy-start(f32[768]{0:T(1024)S(1)} %rsqrt.13) | copy-start | bytes 9220
  40.2 11.7 %copy-start.38 = (f32[768]{0:T(1024)}, f32[768]{0:T(1024)S(1)}, u32[]{:S(2)}) copy-start(f32[768]{0:T(1024)S(1)} %convert_element_type.233) | copy-start | bytes 9220
  40.2 11.7 %copy-start.53 = (pred[768]{0:T(1024)(128)(4,1)}, pred[768]{0:T(1024)(128)(4,1)S(1)}, u32[]{:S(2)}) copy-start(pred[768]{0:T(1024)(128)(4,1)S(1)} %get-tuple-element.351) | copy-start | bytes 2308
  40.2 11.7 %copy-start.55 = (pred[768]{0:T(1024)(128)(4,1)}, pred[768]{0:T(1024)(128)(4,1)S(1)}, u32[]{:S(2)}) copy-start(pred[768]{0:T(1024)(128)(4,1)S(1)} %get-tuple-element.352) | copy-start | bytes 2308
  40.7 11.2 %copy-start.41 = (s32[768]{0:T(1024)}, s32[768]{0:T(1024)S(1)}, u32[]{:S(2)}) copy-start(s32[768]{0:T(1024)S(1)} %get-tuple-element.349) | copy-start | bytes 9220
  40.7 11.2 %copy-start.44 = (s32[768]{0:T(1024)}, s32[768]{0:T(1024)S(1)}, u32[]{:S(2)}) copy-start(s32[768]{0:T(1024)S(1)} %get-tuple-element.350) | copy-start | bytes 9220
  40.8 11.2 %copy-start.47 = (f32[768]{0:T(1024)}, f32[768]{0:T(1024)S(1)}, u32[]{:S(2)}) copy-start(f32[768]{0:T(1024)S(1)} %select_reduce_fusion) | copy-start | bytes 9220
  42.5 9.4 %copy-start.7 = (bf16[768,768]{1,0:T(8,128)(2,1)}, bf16[768,768]{1,0:T(8,128)(2,1)S(1)}, u32[]{:S(2)}) copy-start(bf16[768,768]{1,0:T(8,128)(2,1)S(1)} %get-tuple-element.338) | copy-start | bytes 3538948
  51.9 16.4 %copy-start.22 = (f32[768,2304]{1,0:T(8,128)}, f32[768,2304]{1,0:T(8,128)S(1)}, u32[]{:S(2)}) copy-start(f32[768,2304]{1,0:T(8,128)S(1)} %convolution_add_fusion) | copy-start | bytes 21233668
  68.3 9.5 %copy-start.3 = (bf16[3,256,768]{2,1,0:T(8,128)(2,1)S(1)}, bf16[3,256,768]{2,1,0:T(8,128)(2,1)}, u32[]{:S(2)}) copy-start(bf16[3,256,768]{2,1,0:T(8,128)(2,1)} %param.33) | copy-start | bytes 3538948
  68.3 83.7 %all-gather.12.cloned.1.call-start = ((), (), s32[]{:S(2)}) async-start(), calls=%async_computation.8 | async-start | bytes 5898240 | tf_op jit(solution)/shard_map/all_gather | solution.py:216
  71.3 244.4 %all-gather.16.cloned.1.call-start = ((), (), s32[]{:S(2)}) async-start(), calls=%async_computation.10 | async-start | bytes 5308416 | tf_op jit(solution)/shard_map/all_gather | solution.py:169
  71.9 252.8 %all-gather.18.cloned.1.call-start = ((), (), s32[]{:S(2)}) async-start(), calls=%async_computation.11 | async-start | bytes 5308416 | tf_op jit(solution)/shard_map/all_gather | solution.py:171
  72.5 339.2 %reduce-scatter.7.cloned.1.call-start = ((), (), s32[]{:S(2)}) async-start(), calls=%async_computation.12 | async-start | bytes 5898240 | tf_op jit(solution)/shard_map/reduce_scatter | solution.py:280
  119.2 39.5 %copy-start.18 = (bf16[3,1,12,256,64]{3,4,2,1,0:T(8,128)(2,1)S(1)}, bf16[3,1,12,256,64]{3,4,2,1,0:T(8,128)(2,1)}, u32[]{:S(2)}) copy-start(bf16[3,1,12,256,64]{3,4,2,1,0:T(8,128)(2,1)} %custom-call) | copy-start | bytes 3538948
  299.2 128.9 %reduce-scatter.9.cloned.1.call-start = ((), (), s32[]{:S(2)}) async-start(), calls=%async_computation.13 | async-start | bytes 5898240 | tf_op jit(solution)/shard_map/reduce_scatter | solution.py:283
  305.9 9.8 %copy-start.9 = (bf16[768,768]{1,0:T(8,128)(2,1)S(1)}, bf16[768,768]{1,0:T(8,128)(2,1)}, u32[]{:S(2)}) copy-start(bf16[768,768]{1,0:T(8,128)(2,1)} %get-tuple-element.339) | copy-start | bytes 3538948
  305.9 157.5 %reduce-scatter.13.cloned.1.call-start = ((), (), s32[]{:S(2)}) async-start(), calls=%async_computation.15 | async-start | bytes 1327104 | tf_op jit(solution)/shard_map/reduce_scatter | solution.py:319
  315.7 9.0 %copy-start.4 = (bf16[3,256,768]{2,1,0:T(8,128)(2,1)S(1)}, bf16[3,256,768]{2,1,0:T(8,128)(2,1)}, u32[]{:S(2)}) copy-start(bf16[3,256,768]{2,1,0:T(8,128)(2,1)} %param.33) | copy-start | bytes 3538948
  324.7 29.5 %copy-start.20 = (bf16[3,1,12,256,64]{3,4,2,1,0:T(8,128)(2,1)S(1)}, bf16[3,1,12,256,64]{3,4,2,1,0:T(8,128)(2,1)}, u32[]{:S(2)}) copy-start(bf16[3,1,12,256,64]{3,4,2,1,0:T(8,128)(2,1)} %copy-done.19) | copy-start | bytes 3538948
  357.7 138.6 %reduce-scatter.17.cloned.1.call-start = ((), (), s32[]{:S(2)}) async-start(), calls=%async_computation.17 | async-start | bytes 5308416 | tf_op jit(solution)/shard_map/reduce_scatter | solution.py:337
  378.1 175.5 %reduce-scatter.15.cloned.1.call-start = ((), (), s32[]{:S(2)}) async-start(), calls=%async_computation.16 | async-start | bytes 5308416 | tf_op jit(solution)/shard_map/reduce_scatter | solution.py:331
  386.4 219.1 %reduce-scatter.11.cloned.1.call-start = ((), (), s32[]{:S(2)}) async-start(), calls=%async_computation.14 | async-start | bytes 3981312 | tf_op jit(solution)/shard_map/reduce_scatter | solution.py:313
  411.6 16.4 %copy-start.8 = (bf16[768,768]{1,0:T(8,128)(2,1)S(1)}, bf16[768,768]{1,0:T(8,128)(2,1)}, u32[]{:S(2)}) copy-start(bf16[768,768]{1,0:T(8,128)(2,1)} %copy-done.7) | copy-start | bytes 3538948
  411.6 16.4 %copy-start.13 = (bf16[768,768]{1,0:T(8,128)(2,1)S(1)}, bf16[768,768]{1,0:T(8,128)(2,1)}, u32[]{:S(2)}) copy-start(bf16[768,768]{1,0:T(8,128)(2,1)} %fusion.88) | copy-start | bytes 3538948
  434.5 250.6 %all-reduce.20.cloned.1.call-start = ((), (), s32[]{:S(2)}) async-start(), calls=%async_computation.18 | async-start | bytes 3538944 | tf_op jit(solution)/shard_map/psum | solution.py:361
  447.4 10.0 %copy-start.1 = (bf16[3,256,768]{2,1,0:T(8,128)(2,1)S(1)}, bf16[3,256,768]{2,1,0:T(8,128)(2,1)}, u32[]{:S(2)}) copy-start(bf16[3,256,768]{2,1,0:T(8,128)(2,1)} %param.19) | copy-start | bytes 3538948
  447.4 10.0 %copy-start.11 = (bf16[3,256,768]{2,1,0:T(8,128)(2,1)S(1)}, bf16[3,256,768]{2,1,0:T(8,128)(2,1)}, u32[]{:S(2)}) copy-start(bf16[3,256,768]{2,1,0:T(8,128)(2,1)} %reduce-scatter.9.cloned.1.call-done) | copy-start | bytes 3538948
  447.4 10.0 %copy-start.14 = (bf16[768,768]{1,0:T(8,128)(2,1)S(1)}, bf16[768,768]{1,0:T(8,128)(2,1)}, u32[]{:S(2)}) copy-start(bf16[768,768]{1,0:T(8,128)(2,1)} %fusion.88) | copy-start | bytes 3538948
  447.4 10.0 %copy-start.16 = (bf16[768,768]{1,0:T(8,128)(2,1)S(1)}, bf16[768,768]{1,0:T(8,128)(2,1)}, u32[]{:S(2)}) copy-start(bf16[768,768]{1,0:T(8,128)(2,1)} %fusion.90) | copy-start | bytes 3538948
  447.4 10.0 %copy-start.25 = (f32[768]{0:T(1024)S(1)}, f32[768]{0:T(1024)}, u32[]{:S(2)}) copy-start(f32[768]{0:T(1024)} %copy-done.24) | copy-start | bytes 9220
  447.5 10.0 %copy-start.27 = (f32[768]{0:T(1024)S(1)}, f32[768]{0:T(1024)}, u32[]{:S(2)}) copy-start(f32[768]{0:T(1024)} %copy-done.26) | copy-start | bytes 9220
  447.5 10.0 %copy-start.29 = (f32[768]{0:T(1024)S(1)}, f32[768]{0:T(1024)}, u32[]{:S(2)}) copy-start(f32[768]{0:T(1024)} %copy-done.28) | copy-start | bytes 9220
  447.5 10.0 %copy-start.57 = (bf16[768,2304]{1,0:T(8,128)(2,1)S(1)}, bf16[768,2304]{1,0:T(8,128)(2,1)}, u32[]{:S(2)}) copy-start(bf16[768,2304]{1,0:T(8,128)(2,1)} %all-gather.8.cloned.1.call-done) | copy-start | bytes 10616836
  457.5 148.1 %copy-start.31 = (f32[768]{0:T(1024)S(1)}, f32[768]{0:T(1024)}, u32[]{:S(2)}) copy-start(f32[768]{0:T(1024)} %copy-done.30) | copy-start | bytes 9220
  685.1 6.1 copy-start.66
  (32 other events, 96.7 us)
Sparse Core Ops, SparseCore 0:
  10.0 36.9 all-gather.7
  48.8 24.0 all-gather.13
  75.0 37.4 all-gather.9
  114.5 37.4 all-gather.11
  153.8 38.9 all-gather.15
  194.5 38.9 all-gather.17
  299.3 48.1 reduce-scatter.6
  350.2 47.8 reduce-scatter.8
  401.9 36.7 reduce-scatter.12
  442.4 53.8 reduce-scatter.16
  499.7 53.8 reduce-scatter.14
  557.4 48.0 reduce-scatter.10
  608.4 76.6 all-reduce.19
where the time goes:
time: 704 us; the launch traced here: 699 us
  matrix products  262 us (37%)
  waiting for transfers between devices  195 us (28%)
  blocking collectives  79 us (11%)
  other arithmetic  78.4 us (11%)
  local copies, waits for them, and re-layouts  64.6 us (9%)
  between operations  18.6 us (3%)
    dot_general x4, matrix products, rotate_wide(): swapped = jnp.dot(rows_in, swapper, precision=highest)  69.8 us
    reduce_scatter x1, waiting for transfers between devices, shards(): lax.psum_scatter(grad_w_fc.astype(jnp.bfloat16), ('fsdp', 'ctx'), scatter...  57.4 us
    reduce_scatter x1, waiting for transfers between devices, shards(): lax.psum_scatter(grad_w_qkv.astype(jnp.bfloat16), ('fsdp', 'ctx'), scatte...  51.8 us
    unnamed x2, blocking collectives  51.6 us
    dot_general x4, matrix products, trans_right(): lax.dot_general(matrix_a, matrix_b, (((1,), (1,)), ((), ())), preferred_e...  44.4 us
    reduce_scatter x1, waiting for transfers between devices, shards(): lax.psum_scatter(grad_w_proj.astype(jnp.bfloat16), ('fsdp', 'ctx'), scatt...  32.9 us
    all_gather x1, waiting for transfers between devices, shards(): lax.all_gather(value_seq, 'ctx', axis=1, tiled=True)  32.8 us
    dot_general x3, matrix products, score_grads(): jnp.einsum('phqd,phkd->phqk', grad_combined, value_part, preferred_elemen...  26.3 us
  transfers between devices with their start and end apart: 13, of which 7 were waited for; matrix products, arithmetic and copies ran while one was open for 56% of the time, Pallas kernels for 0%

commit v1 on v0

v1 whole, which is shorter than its diff:
```python
from functools import partial
import math

import jax
import jax.numpy as jnp
import numpy as np
from jax import lax
from jax.experimental import pallas as pl
from jax.experimental.pallas import tpu as pltpu
from jax.sharding import PartitionSpec as P

HEADS = 12
HEAD = 64
ROT = 16

epsilon = 1e-05
far_below = -1e30
low = jnp.bfloat16
wide = jnp.float32
log2e = math.log2(math.e)


def nn(a, b):
    return lax.dot_general(a, b, (((1,), (0,)), ((), ())), preferred_element_type=wide)


def nt(a, b):
    return lax.dot_general(a, b, (((1,), (1,)), ((), ())), preferred_element_type=wide)


def swap(value, axis, bits):
    size = lax.axis_size(axis)
    return lax.ppermute(value, axis, [(i, i ^ bits) for i in range(size)])


def in_order(rel, me):
    out = []
    for k in range(len(rel)):
        value = rel[k]
        for m in range(1, len(rel)):
            value = jnp.where(me == m, rel[k ^ m], value)
        out.append(value)
    return out


def pick(stacked, index):
    return lax.dynamic_index_in_dim(stacked, index, 0, keepdims=False)


def row_norm(block):
    values = block.astype(wide)
    center = values - jnp.mean(values, axis=-1, keepdims=True)
    spread = jnp.mean(center * center, axis=-1, keepdims=True)
    return center * lax.rsqrt(spread + epsilon)


def gelu_parts(v):
    bell = jnp.exp2(v * v * (-0.5 * log2e))
    base = 1.0 + (0.3275911 / math.sqrt(2.0)) * jnp.abs(v)
    t = pl.reciprocal(base, approx=True)
    t = t * (2.0 - base * t)
    poly = 0.5 * 1.061405429
    for coef in (-1.453152027, 1.421413741, -0.284496736, 0.254829592):
        poly = poly * t + 0.5 * coef
    tail = poly * t * bell
    phi = jnp.where(v >= 0, 1.0 - tail, tail)
    return phi, phi + v * bell * (1.0 / math.sqrt(2.0 * math.pi))


def ff_kernel(blocks, first_call, *refs):
    x_refs, refs = refs[:blocks], refs[blocks:]
    c_refs, refs = refs[:blocks], refs[blocks:]
    fc, proj, gain, shift, bias = refs[:5]
    refs = refs[5:]
    if not first_call:
        acc_fc, acc_proj, acc_vec = refs[:3]
        refs = refs[3:]
    outp, ep, dfc, dproj, vec, sec_s, hid_s, gp_s, cot_s, n_s = refs
    rows = x_refs[0].shape[0]
    hidden = fc.shape[1]
    dgain = jnp.zeros((1, fc.shape[0]), wide)
    dshift = jnp.zeros((1, fc.shape[0]), wide)
    dbias = jnp.zeros((1, hidden), wide)
    for j in range(blocks):
        here = pl.ds(j * rows, rows)
        n = row_norm(x_refs[j][...])
        second = (n * gain[...] + shift[...]).astype(low)
        sec_s[here, :] = second
        cot = c_refs[j][...]
        cot_s[here, :] = cot
        pre = nn(second, fc[...]) + bias[...]
        phi, slope = gelu_parts(pre)
        hid = (pre * phi).astype(low)
        gp = nt(cot, proj[...]) * slope
        dbias = dbias + jnp.sum(gp, axis=0, keepdims=True)
        gp = gp.astype(low)
        hid_s[here, :] = hid
        gp_s[here, :] = gp
        outp[j] = nn(hid, proj[...]).astype(outp.dtype)
        dsec = nt(gp, fc[...])
        dgain = dgain + jnp.sum(dsec * n, axis=0, keepdims=True)
        dshift = dshift + jnp.sum(dsec, axis=0, keepdims=True)
        ep[j] = (dsec * gain[...]).astype(ep.dtype)
    w_fc = nn(jnp.transpose(sec_s[...]), gp_s[...])
    w_proj = nn(jnp.transpose(hid_s[...]), cot_s[...])
    if not first_call:
        w_fc = w_fc + acc_fc[...]
        w_proj = w_proj + acc_proj[...]
        dgain = dgain + acc_vec[0:1, :]
        dshift = dshift + acc_vec[1:2, :]
        dbias = dbias + acc_vec[2:3, :]
    dfc[...] = w_fc
    dproj[...] = w_proj
    vec[0:1, :] = dgain
    vec[1:2, :] = dshift
    vec[2:3, :] = dbias


def ff_call(xs, cots, fc, proj, gain, shift, bias, acc):
    blocks, (rows, features) = len(xs), xs[0].shape
    hidden = fc.shape[1]
    total = blocks * rows
    first_call = acc is None
    operands = [*xs, *cots, fc, proj, gain, shift, bias] + ([] if first_call else list(acc))
    vmem = pl.BlockSpec(memory_space=pltpu.VMEM)
    aliases = {} if first_call else {2 * blocks + 5 + k: 2 + k for k in range(3)}
    return pl.pallas_call(
        partial(ff_kernel, blocks, first_call),
        out_shape=(
            jax.ShapeDtypeStruct((blocks, rows, features), low),
            jax.ShapeDtypeStruct((blocks, rows, features), low),
            jax.ShapeDtypeStruct((features, hidden), wide),
            jax.ShapeDtypeStruct((hidden, features), wide),
            jax.ShapeDtypeStruct((8, features), wide),
        ),
        in_specs=[vmem] * len(operands),
        out_specs=(vmem,) * 5,
        scratch_shapes=[
            pltpu.VMEM((total, features), low),
            pltpu.VMEM((total, hidden), low),
            pltpu.VMEM((total, hidden), low),
            pltpu.VMEM((total, features), low),
            pltpu.VMEM((8, features), wide),
        ],
        input_output_aliases=aliases,
        compiler_params=pltpu.CompilerParams(vmem_limit_bytes=44 * 2**20),
        cost_estimate=pl.CostEstimate(
            flops=12 * total * features * hidden,
            bytes_accessed=30 * 2**20,
            transcendentals=total * hidden,
        ),
        name="feed_forward",
    )(*operands)


def turn(block, cosine, sine):
    half = ROT // 2
    a, b = block[0:half], block[half:ROT]
    return jnp.concatenate(
        [a * cosine - b * sine, b * cosine + a * sine, block[ROT:]], axis=0
    )


def att_kernel(blocks, heads, first_call, *refs):
    me_ref, refs = refs[0], refs[1:]
    x_refs, refs = refs[:blocks], refs[blocks:]
    c_refs, refs = refs[:blocks], refs[blocks:]
    w, bias, wout, gain, shift, seg, cosine, sine, outp, ep = refs[:10]
    refs = refs[10:]
    if not first_call:
        acc_w, acc_o, acc_vec = refs[:3]
        refs = refs[3:]
    out_keep, out_send, e_keep, e_send, dw, dwo, vec = refs[:7]
    first_s, n_s, cot_s, wt_s, qt_s, kt_s, vt_s, k_s, v_s, dot_s, mask_s, att_s, d_s, dk_s, dv_s = refs[7:]
    me = me_ref[0]
    rows, features = x_refs[0].shape
    length = blocks * rows
    part = heads * HEAD
    reach = length // 2
    scale = 1.0 / math.sqrt(HEAD)

    wt_s[...] = jnp.transpose(w[...])

    seg_row = seg[...]
    seg_col = jnp.transpose(jnp.broadcast_to(seg_row, (128, length)))
    spans, place = [], 0
    for i in range(blocks):
        start = max(0, i * rows - reach)
        count = (i + 1) * rows - start
        spans.append((start, count, place))
        ours = seg_row[:, i * rows : (i + 1) * rows]
        theirs = seg_col[start : start + count]
        theirs = jnp.concatenate([theirs] * (rows // 128), axis=1)
        key = start + lax.broadcasted_iota(jnp.int32, (count, rows), 0)
        query = i * rows + lax.broadcasted_iota(jnp.int32, (count, rows), 1)
        allowed = (theirs == ours) & (key <= query)
        mask_s[place : place + count, :] = jnp.where(allowed, 0.0, far_below)
        place += count

    for j in range(blocks):
        off = pl.multiple_of((me ^ j) * rows, rows)
        n = row_norm(x_refs[j][...])
        n_s[pl.ds(off, rows), :] = n.astype(low)
        first = (n * gain[...] + shift[...]).astype(low)
        first_s[pl.ds(off, rows), :] = first
        cot = c_refs[j][...]
        cot_s[pl.ds(off, rows), :] = cot
        cos_b, sin_b = cosine[:, pl.ds(off, rows)], sine[:, pl.ds(off, rows)]
        made = nt(wt_s[...], first) + bias[...]
        for h in range(heads):
            lo, hi = h * HEAD, (h + 1) * HEAD
            query = turn(made[lo:hi], cos_b, sin_b).astype(low)
            qt_s[lo:hi, pl.ds(off, rows)] = (query.astype(wide) * scale).astype(low)
            key = turn(made[part + lo : part + hi], cos_b, sin_b).astype(low)
            kt_s[lo:hi, pl.ds(off, rows)] = key
            value = made[2 * part + lo : 2 * part + hi].astype(low)
            vt_s[lo:hi, pl.ds(off, rows)] = value
            k_s[h, pl.ds(off, rows), :] = jnp.transpose(key)
            v_s[h, pl.ds(off, rows), :] = jnp.transpose(value)
        dot_s[:, pl.ds(off, rows)] = nt(wout[...], cot).astype(low)

    dk_s[...] = jnp.zeros_like(dk_s)
    dv_s[...] = jnp.zeros_like(dv_s)

    def one_head(h, carry):
        base = pl.multiple_of(h * HEAD, HEAD)
        mine = pl.ds(base, HEAD)
        for i in range(blocks):
            start, count, place = spans[i]
            here, there = slice(i * rows, (i + 1) * rows), slice(start, start + count)
            query, grad = qt_s[mine, here], dot_s[mine, here]
            score = nn(k_s[h, there, :], query) + mask_s[place : place + count, :]
            top = jnp.max(score, axis=0, keepdims=True)
            lifted = jnp.exp2((score - top) * log2e)
            total = jnp.sum(lifted, axis=0, keepdims=True)
            prob = lifted * (1.0 / total)
            prob_low = prob.astype(low)
            att_s[mine, here] = nn(vt_s[mine, there], prob_low).astype(low)
            dprob = nn(v_s[h, there, :], grad)
            inner = jnp.sum(prob * dprob, axis=0, keepdims=True)
            dscore = (prob * (dprob - inner)).astype(low)
            dv_s[mine, there] += nt(grad, prob_low)
            dk_s[mine, there] += nt(query, dscore)
            dq = nn(kt_s[mine, there], dscore) * scale
            cos_b, sin_b = cosine[:, here], sine[:, here]
            d_s[mine, here] = turn(dq, cos_b, -sin_b).astype(low)
        return carry

    lax.fori_loop(0, heads, one_head, 0)
    for h in range(heads):
        lo, hi = h * HEAD, (h + 1) * HEAD
        d_s[part + lo : part + hi, :] = turn(dk_s[lo:hi, :], cosine[...], -sine[...]).astype(low)
    d_s[2 * part : 3 * part, :] = dv_s[...].astype(low)

    dgain = jnp.zeros((1, features), wide)
    dshift = jnp.zeros((1, features), wide)
    dbias = jnp.zeros((8, 3 * part), wide)
    for j in range(blocks):
        off = pl.multiple_of((me ^ j) * rows, rows)
        att = jnp.transpose(att_s[:, pl.ds(off, rows)])
        out = nn(att, wout[...]) + outp[j].astype(wide)
        dqkv = jnp.transpose(d_s[:, pl.ds(off, rows)])
        dbias = dbias + nn(jnp.ones((8, rows), low), dqkv)
        dfirst = nn(dqkv, wt_s[...])
        n = n_s[pl.ds(off, rows), :].astype(wide)
        dgain = dgain + jnp.sum(dfirst * n, axis=0, keepdims=True)
        dshift = dshift + jnp.sum(dfirst, axis=0, keepdims=True)
        e = dfirst * gain[...] + ep[j].astype(wide)
        (out_send if j % 2 else out_keep)[j // 2] = out.astype(low)
        (e_send if j % 2 else e_keep)[j // 2] = e.astype(low)
    g_w = nn(d_s[...], first_s[...])
    g_o = nn(att_s[...], cot_s[...])
    dbias = dbias[0:1]
    if not first_call:
        g_w = g_w + acc_w[...]
        g_o = g_o + acc_o[...]
        dgain = dgain + acc_vec[0:1, :]
        dshift = dshift + acc_vec[1:2, :]
        dbias = dbias + acc_vec[2:3, 0 : 3 * part]
    dw[...] = g_w
    dwo[...] = g_o
    vec[0:1, :] = dgain
    vec[1:2, :] = dshift
    vec[2:3, 0 : 3 * part] = dbias


def att_call(me, xs, cots, w, bias, wout, gain, shift, seg, cosine, sine, outp, ep, acc):
    blocks, (rows, features) = len(xs), xs[0].shape
    part = wout.shape[0]
    heads = part // HEAD
    length = blocks * rows
    first_call = acc is None
    operands = [me, *xs, *cots, w, bias, wout, gain, shift, seg, cosine, sine, outp, ep]
    base = len(operands)
    operands += [] if first_call else list(acc)
    vmem = pl.BlockSpec(memory_space=pltpu.VMEM)
    aliases = {} if first_call else {base + k: 4 + k for k in range(3)}
    half = jax.ShapeDtypeStruct((blocks // 2, rows, features), low)
    reach = length // 2
    masked = sum((i + 1) * rows - max(0, i * rows - reach) for i in range(blocks))
    return pl.pallas_call(
        partial(att_kernel, blocks, heads, first_call),
        out_shape=(
            half,
            half,
            half,
            half,
            jax.ShapeDtypeStruct((3 * part, features), wide),
            jax.ShapeDtypeStruct((part, features), wide),
            jax.ShapeDtypeStruct((8, features), wide),
        ),
        in_specs=[pl.BlockSpec(memory_space=pltpu.SMEM)] + [vmem] * (len(operands) - 1),
        out_specs=(vmem,) * 7,
        scratch_shapes=[
            pltpu.VMEM((length, features), low),
            pltpu.VMEM((length, features), low),
            pltpu.VMEM((length, features), low),
            pltpu.VMEM((3 * part, features), low),
            pltpu.VMEM((part, length), low),
            pltpu.VMEM((part, length), low),
            pltpu.VMEM((part, length), low),
            pltpu.VMEM((heads, length, HEAD), low),
            pltpu.VMEM((heads, length, HEAD), low),
            pltpu.VMEM((part, length), low),
            pltpu.VMEM((masked, rows), wide),
            pltpu.VMEM((part, length), low),
            pltpu.VMEM((3 * part, length), low),
            pltpu.VMEM((part, length), wide),
            pltpu.VMEM((part, length), wide),
        ],
        input_output_aliases=aliases,
        compiler_params=pltpu.CompilerParams(vmem_limit_bytes=50 * 2**20),
        cost_estimate=pl.CostEstimate(
            flops=24 * length * features * part + 12 * heads * masked * rows * 256,
            bytes_accessed=30 * 2**20,
            transcendentals=heads * masked * rows,
        ),
        name="attention",
    )(*operands)


def shards(
    tokens,
    segment,
    ln1_gain,
    ln1_bias,
    qkv_weight,
    qkv_bias,
    out_weight,
    out_bias,
    ln2_gain,
    ln2_bias,
    fc_weight,
    fc_bias,
    proj_weight,
    proj_bias,
    cotangent,
):
    ctx, fsdp, rep = lax.axis_size("ctx"), lax.axis_size("fsdp"), lax.axis_size("rep")
    c, f, r = lax.axis_index("ctx"), lax.axis_index("fsdp"), lax.axis_index("rep")
    paired = fsdp == 2 and ctx == 4 and rep == 4
    seqs, local_len, features = tokens.shape
    length = local_len * ctx
    owned = qkv_weight.shape[0]
    hidden_own = proj_weight.shape[0]
    hidden_all = fc_weight.shape[1]
    hidden = hidden_all // ctx
    part = features // ctx
    me = f * ctx + c

    def head_block(index):
        return ((index & 1) << 1) | (index >> 1) if paired else index

    vectors = (ln1_gain, ln1_bias, ln2_gain, ln2_bias, out_bias, proj_bias, qkv_bias, fc_bias)
    if paired:
        placed = jnp.concatenate(
            [
                lax.dynamic_update_slice(
                    jnp.zeros((v.shape[0] * fsdp * ctx,), low), v, (me * v.shape[0],)
                )
                for v in vectors
            ]
        ).reshape(-1, 128)
        for axis, bits in (("ctx", 2), ("ctx", 1), ("fsdp", 1)):
            placed = placed + swap(placed, axis, bits)
        placed = placed.reshape(-1)
        ends = np.cumsum([0] + [v.shape[0] * fsdp * ctx for v in vectors])
        vectors = [placed[int(a) : int(b)] for a, b in zip(ends[:-1], ends[1:])]
    else:
        vectors = [lax.all_gather(v, ("fsdp", "ctx"), axis=0, tiled=True) for v in vectors]
    gain_one, shift_one, gain_two, shift_two, b_out, b_proj, b_qkv, b_fc = [
        v.astype(wide) for v in vectors
    ]
    b_qkv = pick(b_qkv.reshape(3, ctx, part).transpose(1, 0, 2), head_block(c)).reshape(3 * part, 1)
    b_fc = pick(b_fc.reshape(fsdp, ctx, hidden_own).transpose(1, 0, 2), c).reshape(1, hidden)
    gain_one, shift_one, gain_two, shift_two = [
        v.reshape(1, features) for v in (gain_one, shift_one, gain_two, shift_two)
    ]

    qkv_cols = qkv_weight.reshape(owned, 3, ctx, part).transpose(2, 0, 1, 3).reshape(ctx, owned, 3 * part)
    fc_cols = fc_weight.reshape(owned, fsdp, ctx, hidden_own).transpose(2, 0, 1, 3).reshape(ctx, owned, hidden)

    def gather_columns(cols, block_of):
        rel = [pick(cols, block_of(c))]
        rel += [swap(pick(cols, block_of(c ^ k)), "ctx", k) for k in range(1, ctx)]
        mine = jnp.stack(in_order(rel, c))
        whole = in_order([mine, swap(mine, "fsdp", 1)], f)
        return jnp.stack(whole).reshape(features, cols.shape[2])

    def gather_columns_any(cols, block_of):
        whole = lax.all_gather(cols, ("fsdp", "ctx"), axis=1, tiled=True)
        return pick(whole, block_of(c))

    gather = gather_columns if paired else gather_columns_any
    w_qkv = gather(qkv_cols, head_block)
    w_fc = gather(fc_cols, lambda index: index)
    core = c & 1
    if paired:
        pair = jnp.concatenate(in_order([out_weight, swap(out_weight, "ctx", 1)], core))
        across = lax.ppermute(
            pair,
            ("fsdp", "ctx"),
            [((i & 1) * ctx + i, (1 - (i & 1)) * ctx + i) for i in range(ctx)],
        )
        w_out = jnp.where(core == f, pair, across)
        w_proj = jnp.concatenate(in_order([proj_weight, swap(proj_weight, "fsdp", 1)], f))
    else:
        w_out = lax.all_gather(out_weight, ("fsdp", "ctx"), axis=0, tiled=True)
        w_out = pick(w_out.reshape(ctx, part, features), c)
        w_proj = lax.all_gather(proj_weight, "fsdp", axis=0, tiled=True)

    def gather_rows(value):
        over = swap(value, "ctx", 2)
        return [value, swap(value, "ctx", 1), over, swap(over, "ctx", 1)]

    seg_all = jnp.concatenate(in_order(gather_rows(segment.astype(low)), c), axis=1).astype(wide)
    half = ROT // 2
    inverse = (1.0 / np.float32(10000.0) ** (np.arange(0, ROT, 2, dtype=np.float32) / ROT)).astype(np.float32)
    angles = inverse[:, None] * np.arange(length, dtype=np.float32)[None, :]
    cosine, sine = jnp.asarray(np.cos(angles)), jnp.asarray(np.sin(angles))
    me_arr = c.astype(jnp.int32).reshape(1)

    xs, cots = [], []
    for s in range(seqs):
        xs.append(gather_rows(tokens[s]))
        cots.append(gather_rows(cotangent[s]))

    def run_ff(s, acc):
        outp, ep, *acc = ff_call(xs[s], cots[s], w_fc, w_proj, gain_two, shift_two, b_fc, acc)
        return outp, ep, acc

    def run_att(s, outp, ep, acc):
        *parts, a, b, v = att_call(
            me_arr, xs[s], cots[s], w_qkv, b_qkv, w_out, gain_one, shift_one,
            seg_all[s : s + 1], cosine, sine, outp, ep, acc,
        )
        return parts, (a, b, v)

    ff_parts, ff_acc, att_acc, att_parts = [], None, None, []
    for s in range(seqs):
        outp, ep, ff_acc = run_ff(s, ff_acc)
        ff_parts.append((outp, ep))
        if s == 0:
            parts, att_acc = run_att(0, outp, ep, att_acc)
            att_parts.append(parts)
    for s in range(1, seqs):
        parts, att_acc = run_att(s, *ff_parts[s], att_acc)
        att_parts.append(parts)

    def own_rows(keep, send):
        got = swap(send, "ctx", 1)
        both = keep.astype(wide) + got.astype(wide)
        return both[0] + swap(both[1].astype(low), "ctx", 2).astype(wide)

    biases = (b_out + b_proj)[None, :]
    outputs, grads = [], []
    for s in range(seqs):
        out_keep, out_send, e_keep, e_send = att_parts[s]
        x = tokens[s].astype(wide)
        outputs.append((x + own_rows(out_keep, out_send) + biases).astype(low))
        e = own_rows(e_keep, e_send)
        center = x - jnp.mean(x, axis=-1, keepdims=True)
        spread = jnp.mean(center * center, axis=-1, keepdims=True)
        root = lax.rsqrt(spread + epsilon)
        n = center * root
        back = root * (
            e - jnp.mean(e, axis=-1, keepdims=True) - n * jnp.mean(e * n, axis=-1, keepdims=True)
        )
        grads.append((cotangent[s].astype(wide) + back).astype(low))
    output, grad_tokens = jnp.stack(outputs), jnp.stack(grads)

    d_fc, d_proj, ff_vec = ff_acc
    d_qkv, d_out, att_vec = att_acc
    d_qkv = jnp.transpose(d_qkv)

    def across_fsdp(grad):
        parts = grad.reshape(fsdp, -1, grad.shape[1])
        got = swap(pick(parts, 1 - f).astype(low), "fsdp", 1)
        return pick(parts, f) + got.astype(wide)

    def scatter_rep(parts):
        total = pick(parts, r)
        for k in range(1, rep):
            total = total + swap(pick(parts, r ^ k).astype(low), "rep", k).astype(wide)
        return total.astype(low)

    def gather_rep(piece):
        return in_order([piece] + [swap(piece, "rep", k) for k in range(1, rep)], r)

    def reduce_columns(grad):
        cols = grad.shape[1]
        mine = across_fsdp(grad).reshape(ctx, rep, owned // rep, cols)
        total = scatter_rep(mine.transpose(1, 0, 2, 3))
        rel = [pick(total, c)] + [swap(pick(total, c ^ k), "ctx", k) for k in range(1, ctx)]
        return jnp.concatenate(gather_rep(jnp.stack(in_order(rel, c), axis=1)))

    def reduce_rows(mine):
        total = scatter_rep(mine.reshape(rep, -1, mine.shape[1]))
        return jnp.concatenate(gather_rep(total))

    if paired:
        g_fc = reduce_columns(d_fc)
        g_qkv = reduce_columns(d_qkv)
        g_proj = reduce_rows(across_fsdp(d_proj))
        got = lax.ppermute(
            d_out.astype(low),
            ("fsdp", "ctx"),
            [((1 - (i & 1)) * ctx + i, (i & 1) * ctx + i) for i in range(ctx)],
        )
        halves = (d_out + got.astype(wide)).reshape(2, owned, features)
        got = lax.ppermute(
            pick(halves, 1 - core).astype(low),
            ("fsdp", "ctx"),
            [(k * ctx + i, k * ctx + (i ^ 1)) for k in range(fsdp) for i in range(ctx) if (i & 1) == k],
        )
        g_out = reduce_rows(jnp.where(core == f, pick(halves, core), got.astype(wide)))
    else:

        def any_columns(grad):
            grad = lax.psum_scatter(grad.astype(low), "fsdp", scatter_dimension=0, tiled=True)
            grad = lax.psum(grad, "rep")
            return lax.all_to_all(
                grad.reshape(ctx, owned, -1), "ctx", split_axis=0, concat_axis=0
            ).transpose(1, 0, 2)

        g_fc, g_qkv = any_columns(d_fc), any_columns(d_qkv)
        g_proj = lax.psum(
            lax.psum_scatter(d_proj.astype(low), "fsdp", scatter_dimension=0, tiled=True), "rep"
        )
        d_out = jnp.where(jnp.arange(ctx)[:, None, None] == c, d_out[None], 0.0)
        g_out = lax.psum(
            lax.psum_scatter(
                d_out.reshape(features, features).astype(low),
                ("fsdp", "ctx"),
                scatter_dimension=0,
                tiled=True,
            ),
            "rep",
        )
    g_fc = g_fc.reshape(owned, ctx, fsdp, hidden_own).transpose(0, 2, 1, 3).reshape(owned, hidden_all)
    order = [head_block(k) for k in range(ctx)]
    g_qkv = g_qkv.reshape(owned, ctx, 3, part)
    g_qkv = jnp.stack([g_qkv[:, order.index(k)] for k in range(ctx)], axis=2).reshape(owned, 3 * features)

    bias_sum = jnp.sum(cotangent.astype(wide), axis=(0, 1))
    d_b_qkv = jnp.where(
        (jnp.arange(ctx) == head_block(c))[None, :, None],
        att_vec[2, : 3 * part].reshape(3, 1, part),
        0.0,
    ).reshape(-1)
    d_b_fc = jnp.where(
        (jnp.arange(ctx) == c)[None, :, None], ff_vec[2].reshape(fsdp, 1, hidden_own), 0.0
    ).reshape(-1)
    small = (att_vec[0], att_vec[1], ff_vec[0], ff_vec[1], bias_sum, d_b_qkv, d_b_fc)
    summed = jnp.concatenate(small).reshape(-1, 128)
    if paired:
        for axis, bits in (("ctx", 1), ("ctx", 2), ("fsdp", 1), ("rep", 1), ("rep", 2)):
            summed = summed + swap(summed, axis, bits)
    else:
        summed = lax.psum(summed, ("ctx", "fsdp", "rep"))
    summed = summed.reshape(-1)
    ends = np.cumsum([0] + [v.shape[0] for v in small])
    mine = []
    for a, v in zip(ends, small):
        size = v.shape[0] // (fsdp * ctx)
        mine.append(lax.dynamic_slice(summed, (int(a) + me * size,), (size,)))
    g_gain_one, g_shift_one, g_gain_two, g_shift_two, g_bias, g_b_qkv, g_b_fc = mine
    return (
        output,
        grad_tokens,
        g_gain_one,
        g_shift_one,
        g_qkv.astype(wide),
        g_b_qkv,
        g_out.astype(wide),
        g_bias,
        g_gain_two,
        g_shift_two,
        g_fc.astype(wide),
        g_b_fc,
        g_proj.astype(wide),
        g_bias,
    )


def solution(mesh):
    rows, row = P(("rep", "fsdp"), "ctx", None), P(("rep", "fsdp"), "ctx")
    vector, matrix = P(("fsdp", "ctx")), P(("fsdp", "ctx"), None)
    params = (
        vector, vector, matrix, vector, matrix, vector,
        vector, vector, matrix, vector, matrix, vector,
    )
    return jax.shard_map(
        shards,
        mesh=mesh,
        in_specs=(rows, row, *params, rows),
        out_specs=(rows, rows, *params),
        check_vma=False,
    )
```

time: 704 us -> 447 us (0.63)
  matrix products: 262 us -> 0 us
  Pallas kernels: 0 us -> 110 us
  starting transfers between devices: 0.53 us -> 87 us
  blocking collectives: 79 us -> 0 us
  other arithmetic: 78.4 us -> 27.1 us
  waiting for transfers between devices: 195 us -> 147 us
  between operations: 18.6 us -> 2.38 us
    dot_general x37 -> x0, matrix products: 262 us -> none  [the longest x4 69.8 us: rotate_wide(): swapped = jnp.dot(rows_in, swapper, precision=highest)]
    ppermute x0 -> x87, waiting for transfers between devices: none -> 147 us  [the longest x84 137 us: swap(): return lax.ppermute(value, axis, [(i, i ^ bits) for i in range(size)])]
    reduce_scatter x6 -> x0, waiting for transfers between devices: 142 us -> none  [the longest x1 57.4 us: shards(): lax.psum_scatter(grad_w_fc.astype(jnp.bfloat16), ('fsdp', 'ctx'), scatter...]
    pallas_call x0 -> x6, Pallas kernels: none -> 110 us  [the longest x3 68.8 us: att_call(): pl.pallas_call(partial(att_kernel, blocks, heads, first_call), out_shape=...]
    ppermute x0 -> x87, starting transfers between devices: none -> 87 us  [the longest x84 81.8 us: swap(): return lax.ppermute(value, axis, [(i, i ^ bits) for i in range(size)])]
    unnamed x2 -> x0, blocking collectives: 51.6 us -> none
    convert_element_type x27 -> x12, other arithmetic: 52.8 us -> 4.53 us  [the longest x4 2.36 us: scatter_rep(): return total.astype(low)]
    all_gather x6 -> x0, waiting for transfers between devices: 42.5 us -> none  [the longest x1 32.8 us: shards(): lax.all_gather(value_seq, 'ctx', axis=1, tiled=True)]
  transfers between devices with their start and end apart: 13 -> 87, of which waited for: 7 -> 31; matrix products, arithmetic and copies ran while one was open for 56% -> 17% of each run, Pallas kernels for 0% -> 17%
where the time goes in v1:
time: 447 us; the launch traced here: 438 us
  waiting for transfers between devices  147 us (33%)
  Pallas kernels  110 us (25%)
  starting transfers between devices  87 us (19%)
  local copies, waits for them, and re-layouts  64.3 us (14%)
  other arithmetic  27.1 us (6%)
    ppermute x84, waiting for transfers between devices, swap(): return lax.ppermute(value, axis, [(i, i ^ bits) for i in range(size)])  137 us
    ppermute x84, starting transfers between devices, swap(): return lax.ppermute(value, axis, [(i, i ^ bits) for i in range(size)])  81.8 us
    pallas_call x3, Pallas kernels, att_call(): pl.pallas_call(partial(att_kernel, blocks, heads, first_call), out_shape=...  68.8 us
    pallas_call x3, Pallas kernels, ff_call(): pl.pallas_call(partial(ff_kernel, blocks, first_call), out_shape=(jax.Sha...  41.4 us
    unnamed x137, local copies, waits for them, and re-layouts  11.7 us
    ppermute x1, waiting for transfers between devices, shards(): lax.ppermute(pair, ('fsdp', 'ctx'), [((i & 1) * ctx + i, (1 - (i & 1)) *...  10.2 us
  transfers between devices with their start and end apart: 87, of which 31 were waited for; matrix products, arithmetic and copies ran while one was open for 17% of the time, Pallas kernels for 17%

profile of v1, /device:TPU:0, one launch (start us, length us, event | category | flops | bytes accessed | tf_op | source)
XLA Modules:
  0.0 438.2 jit_solution(11688624719585715642)
XLA Ops:
  2.6 2.6 collective-permute-start.1
  15.0 2.4 reshape.308
  17.5 2.1 copy.67
  19.5 2.4 reshape.313
  22.0 2.3 copy.109
  24.3 2.8 reshape.314
  42.1 2.3 collective-permute-done.12
  49.1 3.1 collective-permute-done.18
  52.3 3.0 collective-permute-done.19
  56.8 2.7 collective-permute-start.14
  60.5 10.2 %collective-permute-done.14 = bf16[192,768]{1,0:T(8,128)(2,1)S(1)} collective-permute-done((bf16[192,768]{1,0:T(8,128)(2,1)S(1)}, bf16[192,768]{1,0:T(8,128)(2,1)S(1)}, u32[]{:S(2)}, u32[]{:S(2)}) %collective-permute-start.14) | collective-permute-done | bytes 294944 | tf_op jit(solution)/shard_map/ppermute | solution.py:420
  70.7 2.5 collective-permute-start.22
  74.6 12.7 %collective-permute-done.22 = bf16[384,768]{1,0:T(8,128)(2,1)S(1)} collective-permute-done((bf16[384,768]{1,0:T(8,128)(2,1)S(1)}, bf16[384,768]{1,0:T(8,128)(2,1)S(1)}, u32[]{:S(2)}, u32[]{:S(2)}) %collective-permute-start.22) | collective-permute-done | bytes 589856 | tf_op jit(solution)/shard_map/ppermute | solution.py:33
  90.0 9.4 %collective-permute-done.4.refs_6_.refs_7_ = bf16[256,768]{1,0:T(8,128)(2,1)S(1)} collective-permute-done((bf16[256,768]{1,0:T(8,128)(2,1)S(1)}, bf16[256,768]{1,0:T(8,128)(2,1)S(1)}, u32[]{:S(2)}, u32[]{:S(2)}) %collective-permute-start.4) | collective-permute-done | bytes 393248 | tf_op jit(solution)/shard_map/ppermute | solution.py:33
  100.3 7.5 %collective-permute-done.26.refs_2_.refs_3_ = bf16[256,768]{1,0:T(8,128)(2,1)S(1)} collective-permute-done((bf16[256,768]{1,0:T(8,128)(2,1)S(1)}, bf16[256,768]{1,0:T(8,128)(2,1)S(1)}, u32[]{:S(2)}, u32[]{:S(2)}) %collective-permute-start.26) | collective-permute-done | bytes 393248 | tf_op jit(solution)/shard_map/ppermute | solution.py:33
  108.1 8.1 %collective-permute-done.29.refs_6_.refs_7_ = bf16[256,768]{1,0:T(8,128)(2,1)S(1)} collective-permute-done((bf16[256,768]{1,0:T(8,128)(2,1)S(1)}, bf16[256,768]{1,0:T(8,128)(2,1)S(1)}, u32[]{:S(2)}, u32[]{:S(2)}) %collective-permute-start.29) | collective-permute-done | bytes 393248 | tf_op jit(solution)/shard_map/ppermute | solution.py:33
  117.0 12.0 %feed_forward.3 = (bf16[4,256,768]{2,1,0:T(8,128)(2,1)S(1)}, bf16[4,256,768]{2,1,0:T(8,128)(2,1)S(1)}, f32[768,768]{1,0:T(8,128)}, f32[768,768]{1,0:T(8,128)}, f32[8,768]{1,0:T(8,128)S(1)}) custom-call(bf16[256,768]{1,0:T(8,128)(2,1)S(1)} %get-tuple-element.119.refs_0_.refs_1_, bf16[256,768]{1,0:T(8,128)(2,1)S(1)} %collective-permute-done.refs_1_.refs_2_, ...), custom_call_target="tpu_custom_call" | custom-call | flops 7247757312 | bytes 31457280 | tf_op jit(solution)/shard_map/feed_forward/pallas_call | solution.py:127
  132.5 15.0 %feed_forward.4 = (bf16[4,256,768]{2,1,0:T(8,128)(2,1)S(1)}, bf16[4,256,768]{2,1,0:T(8,128)(2,1)S(1)}, f32[768,768]{1,0:T(8,128)}, f32[768,768]{1,0:T(8,128)}, f32[8,768]{1,0:T(8,128)S(1)}) custom-call(bf16[256,768]{1,0:T(8,128)(2,1)S(1)} %get-tuple-element.121.refs_0_.refs_1_, ...), custom_call_target="tpu_custom_call", output_to_operand_aliasing={{2}: (13, {}), {3}: (14, {}), {4}: (15, {})} | custom-call | flops 7247757312 | bytes 31457280 | tf_op jit(solution)/shard_map/feed_forward/pallas_call | solution.py:127
  149.9 22.5 %attention.3 = (bf16[2,256,768]{2,1,0:T(8,128)(2,1)}, bf16[2,256,768]{2,1,0:T(8,128)(2,1)}, bf16[2,256,768]{2,1,0:T(8,128)(2,1)}, bf16[2,256,768]{2,1,0:T(8,128)...) custom-call(s32[1]{0:T(128)} %bitcast.1.refs_0_, ...), custom_call_target="tpu_custom_call" | custom-call | flops 9059696640 | bytes 31457280 | tf_op jit(solution)/shard_map/attention/pallas_call | solution.py:301
  172.4 23.3 %attention.4 = (bf16[2,256,768]{2,1,0:T(8,128)(2,1)}, bf16[2,256,768]{2,1,0:T(8,128)(2,1)}, bf16[2,256,768]{2,1,0:T(8,128)(2,1)}, bf16[2,256,768]{2,1,0:T(8,128)...) custom-call(s32[1]{0:T(128)} %bitcast.1.refs_0_, ...), custom_call_target="tpu_custom_call", output_to_operand_aliasing={{4}: (19, {}), {5}: (20, {}), {6}: (21, {})} | custom-call | flops 9059696640 | bytes 31457280 | tf_op jit(solution)/shard_map/attention/pallas_call | solution.py:301
  195.7 14.4 %feed_forward.5 = (bf16[4,256,768]{2,1,0:T(8,128)(2,1)S(1)}, bf16[4,256,768]{2,1,0:T(8,128)(2,1)S(1)}, f32[768,768]{1,0:T(8,128)}, f32[768,768]{1,0:T(8,128)}, f32[8,768]{1,0:T(8,128)S(1)}) custom-call(bf16[256,768]{1,0:T(8,128)(2,1)S(1)} %get-tuple-element.120.refs_0_.refs_1_, ...), custom_call_target="tpu_custom_call", output_to_operand_aliasing={{2}: (13, {}), {3}: (14, {}), {4}: (15, {})} | custom-call | flops 7247757312 | bytes 31457280 | tf_op jit(solution)/shard_map/feed_forward/pallas_call | solution.py:127
  212.5 23.0 %attention.5 = (bf16[2,256,768]{2,1,0:T(8,128)(2,1)}, bf16[2,256,768]{2,1,0:T(8,128)(2,1)}, bf16[2,256,768]{2,1,0:T(8,128)(2,1)}, bf16[2,256,768]{2,1,0:T(8,128)...) custom-call(s32[1]{0:T(128)} %bitcast.1.refs_0_, ...), custom_call_target="tpu_custom_call", output_to_operand_aliasing={{4}: (19, {}), {5}: (20, {}), {6}: (21, {})} | custom-call | flops 9059696640 | bytes 31457280 | tf_op jit(solution)/shard_map/attention/pallas_call | solution.py:301
  236.7 2.2 reshape.319
  242.4 2.1 collective-permute-start.52
  245.8 2.8 collective-permute-start.49
  248.5 2.1 fusion.42
  250.7 11.8 %collective-permute-done.49 = f32[72,128]{1,0:T(8,128)S(1)} collective-permute-done((f32[72,128]{1,0:T(8,128)S(1)}, f32[72,128]{1,0:T(8,128)S(1)}, u32[]{:S(2)}, u32[]{:S(2)}) %collective-permute-start.49) | collective-permute-done | bytes 36896 | tf_op jit(solution)/shard_map/ppermute | solution.py:33
  264.1 2.1 fusion.43
  266.5 2.6 collective-permute-start.51
  273.4 4.0 collective-permute-start.66
  279.3 2.9 collective-permute-done.65
  284.4 2.3 collective-permute-start.69
  292.0 2.2 collective-permute-start.53
  295.4 3.4 collective-permute-done.54
  303.0 2.4 collective-permute-start.59
  307.6 10.4 %collective-permute-done.80 = bf16[384,768]{1,0:T(8,128)(2,1)S(1)} collective-permute-done((bf16[384,768]{1,0:T(8,128)(2,1)S(1)}, bf16[384,768]{1,0:T(8,128)(2,1)S(1)}, u32[]{:S(2)}, u32[]{:S(2)}) %collective-permute-start.80) | collective-permute-done | bytes 589856 | tf_op jit(solution)/shard_map/ppermute | solution.py:33
  328.3 2.1 collective-permute-start.83
  330.4 8.8 %collective-permute-done.72 = bf16[4,24,768]{2,1,0:T(8,128)(2,1)} collective-permute-done((bf16[4,24,768]{2,1,0:T(8,128)(2,1)}, bf16[4,24,768]{2,1,0:T(8,128)(2,1)}, u32[]{:S(2)}, u32[]{:S(2)}) %collective-permute-start.72) | collective-permute-done | bytes 147488 | tf_op jit(solution)/shard_map/ppermute | solution.py:33
  339.3 2.5 collective-permute-start.81
  343.1 4.4 %collective-permute-done.82 = bf16[96,768]{1,0:T(8,128)(2,1)S(1)} collective-permute-done((bf16[96,768]{1,0:T(8,128)(2,1)S(1)}, bf16[96,768]{1,0:T(8,128)(2,1)S(1)}, u32[]{:S(2)}, u32[]{:S(2)}) %collective-permute-start.82) | collective-permute-done | bytes 147488 | tf_op jit(solution)/shard_map/ppermute | solution.py:33
  353.2 2.0 collective-permute-start.84
  361.8 2.0 collective-permute-start.77
  368.2 7.2 %collective-permute-start.24 = (bf16[256,768]{1,0:T(8,128)(2,1)}, bf16[256,768]{1,0:T(8,128)(2,1)}, u32[]{:S(2)}, u32[]{:S(2)}) collective-permute-start(bf16[256,768]{1,0:T(8,128)(2,1)} %fusion.45), channel_id=1, source_target_pairs={{0,2},{1,3},{2,0},{3,1},{4,6},{5,7},{6,4},{7,5},{8,10},{9,11},{10,... | collective-permute-start | bytes 1179656 | tf_op jit(solution)/shard_map/ppermute | solution.py:33
  384.1 3.0 copy.87
  387.2 2.8 reshape.335
  389.9 28.8 %collective-permute-done.46 = bf16[256,768]{1,0:T(8,128)(2,1)} collective-permute-done((bf16[256,768]{1,0:T(8,128)(2,1)}, bf16[256,768]{1,0:T(8,128)(2,1)}, u32[]{:S(2)}, u32[]{:S(2)}) %collective-permute-start.46) | collective-permute-done | bytes 393248 | tf_op jit(solution)/shard_map/ppermute | solution.py:33
  422.5 6.9 %collective-permute-done.44 = bf16[256,768]{1,0:T(8,128)(2,1)S(1)} collective-permute-done((bf16[256,768]{1,0:T(8,128)(2,1)}, bf16[256,768]{1,0:T(8,128)(2,1)S(1)}, u32[]{:S(2)}, u32[]{:S(2)}) %collective-permute-start.44) | collective-permute-done | bytes 393248 | tf_op jit(solution)/shard_map/ppermute | solution.py:33
  430.2 2.5 fusion.53
  (428 shorter events, 122.9 us)
Async XLA Ops:
  2.1 85.7 %collective-permute-start = (bf16[256,768]{1,0:T(8,128)(2,1)S(1)}, bf16[256,768]{1,0:T(8,128)(2,1)S(1)}, u32[]{:S(2)}, u32[]{:S(2)}) collective-permute-start(bf16[256,768]{1,0:T(8,128)(2,1)S(1)} %get-tuple-element.119.refs_0_.refs_1_), channel_id=1, source_target_pairs={{0,1},{1,0},{2,3},{3,2},{4,5},{5,4},{6,7},{7,6},{8,9},{9,8},{10,11... | collective-permute-start | bytes 1179656 | tf_op jit(solution)/shard_map/ppermute | solution.py:33
  2.6 85.2 %collective-permute-start.1 = (bf16[256,768]{1,0:T(8,128)(2,1)S(1)}, bf16[256,768]{1,0:T(8,128)(2,1)S(1)}, u32[]{:S(2)}, u32[]{:S(2)}) collective-permute-start(bf16[256,768]{1,0:T(8,128)(2,1)S(1)} %get-tuple-element.119.refs_0_.refs_1_), channel_id=1, source_target_pairs={{0,2},{1,3},{2,0},{3,1},{4,6},{5,7},{6,4},{7,5},{8,10},{9,11},{10,... | collective-permute-start | bytes 1179656 | tf_op jit(solution)/shard_map/ppermute | solution.py:33
  5.2 32.0 %collective-permute-start.15 = (bf16[3,256]{1,0:T(4,128)(2,1)S(1)}, bf16[3,256]{1,0:T(4,128)(2,1)S(1)}, u32[]{:S(2)}, u32[]{:S(2)}) collective-permute-start(bf16[3,256]{1,0:T(4,128)(2,1)S(1)} %convert_element_type.398), channel_id=1, source_target_pairs={{0,2},{1,3},{2,0},{3,1},{4,6},{5,7},{6,4},{7,5},{8,10},{9,11},{10,... | collective-permute-start | bytes 4616 | tf_op jit(solution)/shard_map/ppermute | solution.py:33
  5.3 32.3 %collective-permute-start.17 = (bf16[3,256]{1,0:T(4,128)(2,1)S(1)}, bf16[3,256]{1,0:T(4,128)(2,1)S(1)}, u32[]{:S(2)}, u32[]{:S(2)}) collective-permute-start(bf16[3,256]{1,0:T(4,128)(2,1)S(1)} %convert_element_type.398), channel_id=1, source_target_pairs={{0,1},{1,0},{2,3},{3,2},{4,5},{5,4},{6,7},{7,6},{8,9},{9,8},{10,11... | collective-permute-start | bytes 4616 | tf_op jit(solution)/shard_map/ppermute | solution.py:33
  9.1 28.3 %collective-permute-start.10 = (bf16[78,128]{1,0:T(8,128)(2,1)S(1)}, bf16[78,128]{1,0:T(8,128)(2,1)S(1)}, u32[]{:S(2)}, u32[]{:S(2)}) collective-permute-start(bf16[78,128]{1,0:T(8,128)(2,1)S(1)} %bitcast.465), channel_id=1, source_target_pairs={{0,2},{1,3},{2,0},{3,1},{4,6},{5,7},{6,4},{7,5},{8,10},{9,11},{10,... | collective-permute-start | bytes 59912 | tf_op jit(solution)/shard_map/ppermute | solution.py:33
  52.2 37.5 %collective-permute-start.3 = (bf16[256,768]{1,0:T(8,128)(2,1)S(1)}, bf16[256,768]{1,0:T(8,128)(2,1)S(1)}, u32[]{:S(2)}, u32[]{:S(2)}) collective-permute-start(bf16[256,768]{1,0:T(8,128)(2,1)S(1)} %get-tuple-element.116.refs_4_.refs_5_), channel_id=1, source_target_pairs={{0,1},{1,0},{2,3},{3,2},{4,5},{5,4},{6,7},{7,6},{8,9},{9,8},{10,11... | collective-permute-start | bytes 1179656 | tf_op jit(solution)/shard_map/ppermute | solution.py:33
  55.3 18.0 %collective-permute-start.9 = (bf16[4,96,576]{2,1,0:T(8,128)(2,1)S(1)}, bf16[4,96,576]{2,1,0:T(8,128)(2,1)S(1)}, u32[]{:S(2)}, u32[]{:S(2)}) collective-permute-start(bf16[4,96,576]{2,1,0:T(8,128)(2,1)S(1)} %pad_maximum_fusion.6), channel_id=1, source_target_pairs={{0,4},{4,0},{1,5},{5,1},{2,6},{6,2},{3,7},{7,3},{8,12},{12,8},{9,1... | collective-permute-start | bytes 1327112 | tf_op jit(solution)/shard_map/ppermute | solution.py:33
  56.8 13.9 %collective-permute-start.14 = (bf16[192,768]{1,0:T(8,128)(2,1)S(1)}, bf16[192,768]{1,0:T(8,128)(2,1)S(1)}, u32[]{:S(2)}, u32[]{:S(2)}) collective-permute-start(bf16[192,768]{1,0:T(8,128)(2,1)S(1)} %pad_maximum_fusion.8), channel_id=1, source_target_pairs={{0,4},{5,1},{2,6},{7,3},{8,12},{13,9},{10,14},{15,11},{16,20},{21,... | collective-permute-start | bytes 884744 | tf_op jit(solution)/shard_map/ppermute | solution.py:420
  70.7 16.6 %collective-permute-start.22 = (bf16[384,768]{1,0:T(8,128)(2,1)S(1)}, bf16[384,768]{1,0:T(8,128)(2,1)S(1)}, u32[]{:S(2)}, u32[]{:S(2)}) collective-permute-start(bf16[384,768]{1,0:T(8,128)(2,1)S(1)} %copy-done.37), channel_id=1, source_target_pairs={{0,4},{4,0},{1,5},{5,1},{2,6},{6,2},{3,7},{7,3},{8,12},{12,8},{9,1... | collective-permute-start | bytes 1769480 | tf_op jit(solution)/shard_map/ppermute | solution.py:33
  73.3 26.1 %collective-permute-start.21 = (bf16[4,96,768]{2,1,0:T(8,128)(2,1)S(1)}, bf16[4,96,768]{2,1,0:T(8,128)(2,1)S(1)}, u32[]{:S(2)}, u32[]{:S(2)}) collective-permute-start(bf16[4,96,768]{2,1,0:T(8,128)(2,1)S(1)} %pad_maximum_fusion.5), channel_id=1, source_target_pairs={{0,4},{4,0},{1,5},{5,1},{2,6},{6,2},{3,7},{7,3},{8,12},{12,8},{9,1... | collective-permute-start | bytes 1769480 | tf_op jit(solution)/shard_map/ppermute | solution.py:33
  87.3 12.1 %collective-permute-start.4 = (bf16[256,768]{1,0:T(8,128)(2,1)S(1)}, bf16[256,768]{1,0:T(8,128)(2,1)S(1)}, u32[]{:S(2)}, u32[]{:S(2)}) collective-permute-start(bf16[256,768]{1,0:T(8,128)(2,1)S(1)} %get-tuple-element.116.refs_4_.refs_5_), channel_id=1, source_target_pairs={{0,2},{1,3},{2,0},{3,1},{4,6},{5,7},{6,4},{7,5},{8,10},{9,11},{10,... | collective-permute-start | bytes 1179656 | tf_op jit(solution)/shard_map/ppermute | solution.py:33
  87.8 12.4 %collective-permute-start.25 = (bf16[256,768]{1,0:T(8,128)(2,1)S(1)}, bf16[256,768]{1,0:T(8,128)(2,1)S(1)}, u32[]{:S(2)}, u32[]{:S(2)}) collective-permute-start(bf16[256,768]{1,0:T(8,128)(2,1)S(1)} %get-tuple-element.121.refs_0_.refs_1_), channel_id=1, source_target_pairs={{0,1},{1,0},{2,3},{3,2},{4,5},{5,4},{6,7},{7,6},{8,9},{9,8},{10,11... | collective-permute-start | bytes 1179656 | tf_op jit(solution)/shard_map/ppermute | solution.py:33
  87.9 19.9 %collective-permute-start.26 = (bf16[256,768]{1,0:T(8,128)(2,1)S(1)}, bf16[256,768]{1,0:T(8,128)(2,1)S(1)}, u32[]{:S(2)}, u32[]{:S(2)}) collective-permute-start(bf16[256,768]{1,0:T(8,128)(2,1)S(1)} %get-tuple-element.121.refs_0_.refs_1_), channel_id=1, source_target_pairs={{0,2},{1,3},{2,0},{3,1},{4,6},{5,7},{6,4},{7,5},{8,10},{9,11},{10,... | collective-permute-start | bytes 1179656 | tf_op jit(solution)/shard_map/ppermute | solution.py:33
  89.7 26.5 %collective-permute-start.29 = (bf16[256,768]{1,0:T(8,128)(2,1)S(1)}, bf16[256,768]{1,0:T(8,128)(2,1)S(1)}, u32[]{:S(2)}, u32[]{:S(2)}) collective-permute-start(bf16[256,768]{1,0:T(8,128)(2,1)S(1)} %get-tuple-element.117.refs_4_.refs_5_), channel_id=1, source_target_pairs={{0,2},{1,3},{2,0},{3,1},{4,6},{5,7},{6,4},{7,5},{8,10},{9,11},{10,... | collective-permute-start | bytes 1179656 | tf_op jit(solution)/shard_map/ppermute | solution.py:33
  99.4 17.1 %collective-permute-start.2 = (bf16[256,768]{1,0:T(8,128)(2,1)S(1)}, bf16[256,768]{1,0:T(8,128)(2,1)S(1)}, u32[]{:S(2)}, u32[]{:S(2)}) collective-permute-start(bf16[256,768]{1,0:T(8,128)(2,1)S(1)} %collective-permute-done.1.refs_2_.refs_3_), channel_id=1, source_target_pairs={{0,1},{1,0},{2,3},{3,2},{4,5},{5,4},{6,7},{7,6},{8,9},{9,8},{10,11... | collective-permute-start | bytes 1179656 | tf_op jit(solution)/shard_map/ppermute | solution.py:33
  99.4 17.1 %collective-permute-start.5 = (bf16[256,768]{1,0:T(8,128)(2,1)S(1)}, bf16[256,768]{1,0:T(8,128)(2,1)S(1)}, u32[]{:S(2)}, u32[]{:S(2)}) collective-permute-start(bf16[256,768]{1,0:T(8,128)(2,1)S(1)} %collective-permute-done.4.refs_6_.refs_7_), channel_id=1, source_target_pairs={{0,1},{1,0},{2,3},{3,2},{4,5},{5,4},{6,7},{7,6},{8,9},{9,8},{10,11... | collective-permute-start | bytes 1179656 | tf_op jit(solution)/shard_map/ppermute | solution.py:33
  100.2 31.3 %collective-permute-start.28 = (bf16[256,768]{1,0:T(8,128)(2,1)S(1)}, bf16[256,768]{1,0:T(8,128)(2,1)S(1)}, u32[]{:S(2)}, u32[]{:S(2)}) collective-permute-start(bf16[256,768]{1,0:T(8,128)(2,1)S(1)} %get-tuple-element.117.refs_4_.refs_5_), channel_id=1, source_target_pairs={{0,1},{1,0},{2,3},{3,2},{4,5},{5,4},{6,7},{7,6},{8,9},{9,8},{10,11... | collective-permute-start | bytes 1179656 | tf_op jit(solution)/shard_map/ppermute | solution.py:33
  107.8 23.7 %collective-permute-start.34 = (bf16[256,768]{1,0:T(8,128)(2,1)S(1)}, bf16[256,768]{1,0:T(8,128)(2,1)S(1)}, u32[]{:S(2)}, u32[]{:S(2)}) collective-permute-start(bf16[256,768]{1,0:T(8,128)(2,1)S(1)} %get-tuple-element.120.refs_0_.refs_1_), channel_id=1, source_target_pairs={{0,2},{1,3},{2,0},{3,1},{4,6},{5,7},{6,4},{7,5},{8,10},{9,11},{10,... | collective-permute-start | bytes 1179656 | tf_op jit(solution)/shard_map/ppermute | solution.py:33
  116.2 15.7 %collective-permute-start.37 = (bf16[256,768]{1,0:T(8,128)(2,1)S(1)}, bf16[256,768]{1,0:T(8,128)(2,1)S(1)}, u32[]{:S(2)}, u32[]{:S(2)}) collective-permute-start(bf16[256,768]{1,0:T(8,128)(2,1)S(1)} %get-tuple-element.118.refs_4_.refs_5_), channel_id=1, source_target_pairs={{0,2},{1,3},{2,0},{3,1},{4,6},{5,7},{6,4},{7,5},{8,10},{9,11},{10,... | collective-permute-start | bytes 1179656 | tf_op jit(solution)/shard_map/ppermute | solution.py:33
  116.5 15.5 %collective-permute-start.27 = (bf16[256,768]{1,0:T(8,128)(2,1)S(1)}, bf16[256,768]{1,0:T(8,128)(2,1)S(1)}, u32[]{:S(2)}, u32[]{:S(2)}) collective-permute-start(bf16[256,768]{1,0:T(8,128)(2,1)S(1)} %collective-permute-done.26.refs_2_.refs_3_), channel_id=1, source_target_pairs={{0,1},{1,0},{2,3},{3,2},{4,5},{5,4},{6,7},{7,6},{8,9},{9,8},{10,11... | collective-permute-start | bytes 1179656 | tf_op jit(solution)/shard_map/ppermute | solution.py:33
  116.5 16.0 %collective-permute-start.30 = (bf16[256,768]{1,0:T(8,128)(2,1)S(1)}, bf16[256,768]{1,0:T(8,128)(2,1)S(1)}, u32[]{:S(2)}, u32[]{:S(2)}) collective-permute-start(bf16[256,768]{1,0:T(8,128)(2,1)S(1)} %collective-permute-done.29.refs_6_.refs_7_), channel_id=1, source_target_pairs={{0,1},{1,0},{2,3},{3,2},{4,5},{5,4},{6,7},{7,6},{8,9},{9,8},{10,11... | collective-permute-start | bytes 1179656 | tf_op jit(solution)/shard_map/ppermute | solution.py:33
  131.4 64.3 %collective-permute-start.33 = (bf16[256,768]{1,0:T(8,128)(2,1)S(1)}, bf16[256,768]{1,0:T(8,128)(2,1)S(1)}, u32[]{:S(2)}, u32[]{:S(2)}) collective-permute-start(bf16[256,768]{1,0:T(8,128)(2,1)S(1)} %get-tuple-element.120.refs_0_.refs_1_), channel_id=1, source_target_pairs={{0,1},{1,0},{2,3},{3,2},{4,5},{5,4},{6,7},{7,6},{8,9},{9,8},{10,11... | collective-permute-start | bytes 1179656 | tf_op jit(solution)/shard_map/ppermute | solution.py:33
  131.5 64.2 %collective-permute-start.36 = (bf16[256,768]{1,0:T(8,128)(2,1)S(1)}, bf16[256,768]{1,0:T(8,128)(2,1)S(1)}, u32[]{:S(2)}, u32[]{:S(2)}) collective-permute-start(bf16[256,768]{1,0:T(8,128)(2,1)S(1)} %get-tuple-element.118.refs_4_.refs_5_), channel_id=1, source_target_pairs={{0,1},{1,0},{2,3},{3,2},{4,5},{5,4},{6,7},{7,6},{8,9},{9,8},{10,11... | collective-permute-start | bytes 1179656 | tf_op jit(solution)/shard_map/ppermute | solution.py:33
  132.0 63.8 %collective-permute-start.35 = (bf16[256,768]{1,0:T(8,128)(2,1)S(1)}, bf16[256,768]{1,0:T(8,128)(2,1)S(1)}, u32[]{:S(2)}, u32[]{:S(2)}) collective-permute-start(bf16[256,768]{1,0:T(8,128)(2,1)S(1)} %collective-permute-done.34.refs_2_.refs_3_), channel_id=1, source_target_pairs={{0,1},{1,0},{2,3},{3,2},{4,5},{5,4},{6,7},{7,6},{8,9},{9,8},{10,11... | collective-permute-start | bytes 1179656 | tf_op jit(solution)/shard_map/ppermute | solution.py:33
  132.1 63.7 %collective-permute-start.38 = (bf16[256,768]{1,0:T(8,128)(2,1)S(1)}, bf16[256,768]{1,0:T(8,128)(2,1)S(1)}, u32[]{:S(2)}, u32[]{:S(2)}) collective-permute-start(bf16[256,768]{1,0:T(8,128)(2,1)S(1)} %collective-permute-done.37.refs_6_.refs_7_), channel_id=1, source_target_pairs={{0,1},{1,0},{2,3},{3,2},{4,5},{5,4},{6,7},{7,6},{8,9},{9,8},{10,11... | collective-permute-start | bytes 1179656 | tf_op jit(solution)/shard_map/ppermute | solution.py:33
  235.6 116.6 %collective-permute-start.23 = (bf16[2,256,768]{2,1,0:T(8,128)(2,1)}, bf16[2,256,768]{2,1,0:T(8,128)(2,1)S(1)}, u32[]{:S(2)}, u32[]{:S(2)}) collective-permute-start(bf16[2,256,768]{2,1,0:T(8,128)(2,1)} %get-tuple-element.53), channel_id=1, source_target_pairs={{0,1},{1,0},{2,3},{3,2},{4,5},{5,4},{6,7},{7,6},{8,9},{9,8},{10,11... | collective-permute-start | bytes 2359304 | tf_op jit(solution)/shard_map/ppermute | solution.py:33
  242.4 35.0 %collective-permute-start.52 = (bf16[384,576]{0,1:T(8,128)(2,1)S(1)}, bf16[384,576]{0,1:T(8,128)(2,1)S(1)}, u32[]{:S(2)}, u32[]{:S(2)}) collective-permute-start(bf16[384,576]{0,1:T(8,128)(2,1)S(1)} %bitcast.460), channel_id=1, source_target_pairs={{0,4},{4,0},{1,5},{5,1},{2,6},{6,2},{3,7},{7,3},{8,12},{12,8},{9,1... | collective-permute-start | bytes 1327112 | tf_op jit(solution)/shard_map/ppermute | solution.py:33
  244.5 24.7 %collective-permute-start.62 = (bf16[192,768]{1,0:T(8,128)(2,1)S(1)}, bf16[192,768]{1,0:T(8,128)(2,1)S(1)}, u32[]{:S(2)}, u32[]{:S(2)}) collective-permute-start(bf16[192,768]{1,0:T(8,128)(2,1)S(1)} %convert_element_type.459), channel_id=1, source_target_pairs={{4,0},{1,5},{6,2},{3,7},{12,8},{9,13},{14,10},{11,15},{20,16},{17,... | collective-permute-start | bytes 884744 | tf_op jit(solution)/shard_map/ppermute | solution.py:525
  245.8 16.8 %collective-permute-start.49 = (f32[72,128]{1,0:T(8,128)S(1)}, f32[72,128]{1,0:T(8,128)S(1)}, u32[]{:S(2)}, u32[]{:S(2)}) collective-permute-start(f32[72,128]{1,0:T(8,128)S(1)} %fusion.124), channel_id=1, source_target_pairs={{0,4},{4,0},{1,5},{5,1},{2,6},{6,2},{3,7},{7,3},{8,12},{12,8},{9,1... | collective-permute-start | bytes 110600 | tf_op jit(solution)/shard_map/ppermute | solution.py:33
  250.7 54.7 %collective-permute-start.70 = (bf16[384,768]{1,0:T(8,128)(2,1)}, bf16[384,768]{1,0:T(8,128)(2,1)}, u32[]{:S(2)}, u32[]{:S(2)}) collective-permute-start(bf16[384,768]{1,0:T(8,128)(2,1)} %fusion.42), channel_id=1, source_target_pairs={{0,4},{4,0},{1,5},{5,1},{2,6},{6,2},{3,7},{7,3},{8,12},{12,8},{9,1... | collective-permute-start | bytes 1769480 | tf_op jit(solution)/shard_map/ppermute | solution.py:33
  302.3 51.0 %collective-permute-start.31 = (bf16[2,256,768]{2,1,0:T(8,128)(2,1)}, bf16[2,256,768]{2,1,0:T(8,128)(2,1)}, u32[]{:S(2)}, u32[]{:S(2)}) collective-permute-start(bf16[2,256,768]{2,1,0:T(8,128)(2,1)} %get-tuple-element.63), channel_id=1, source_target_pairs={{0,1},{1,0},{2,3},{3,2},{4,5},{5,4},{6,7},{7,6},{8,9},{9,8},{10,11... | collective-permute-start | bytes 2359304 | tf_op jit(solution)/shard_map/ppermute | solution.py:33
  302.9 15.1 %collective-permute-start.80 = (bf16[384,768]{1,0:T(8,128)(2,1)S(1)}, bf16[384,768]{1,0:T(8,128)(2,1)S(1)}, u32[]{:S(2)}, u32[]{:S(2)}) collective-permute-start(bf16[384,768]{1,0:T(8,128)(2,1)S(1)} %copy-done.38), channel_id=1, source_target_pairs={{0,4},{4,0},{1,5},{5,1},{2,6},{6,2},{3,7},{7,3},{8,12},{12,8},{9,1... | collective-permute-start | bytes 1769480 | tf_op jit(solution)/shard_map/ppermute | solution.py:33
  303.0 16.3 %collective-permute-start.59 = (bf16[24,4,576]{2,0,1:T(8,128)(2,1)S(1)}, bf16[24,4,576]{2,0,1:T(8,128)(2,1)S(1)}, u32[]{:S(2)}, u32[]{:S(2)}) collective-permute-start(bf16[24,4,576]{2,0,1:T(8,128)(2,1)S(1)} %pad_maximum_fusion.10), channel_id=1, source_target_pairs={{0,24},{8,16},{16,8},{24,0},{1,25},{9,17},{17,9},{25,1},{2,26},{10... | collective-permute-start | bytes 331784 | tf_op jit(solution)/shard_map/ppermute | solution.py:33
  305.4 16.0 %collective-permute-start.60 = (bf16[24,4,576]{2,0,1:T(8,128)(2,1)S(1)}, bf16[24,4,576]{2,0,1:T(8,128)(2,1)S(1)}, u32[]{:S(2)}, u32[]{:S(2)}) collective-permute-start(bf16[24,4,576]{2,0,1:T(8,128)(2,1)S(1)} %pad_maximum_fusion.10), channel_id=1, source_target_pairs={{0,16},{8,24},{16,0},{24,8},{1,17},{9,25},{17,1},{25,9},{2,18},{10... | collective-permute-start | bytes 331784 | tf_op jit(solution)/shard_map/ppermute | solution.py:33
  321.4 17.9 %collective-permute-start.72 = (bf16[4,24,768]{2,1,0:T(8,128)(2,1)}, bf16[4,24,768]{2,1,0:T(8,128)(2,1)}, u32[]{:S(2)}, u32[]{:S(2)}) collective-permute-start(bf16[4,24,768]{2,1,0:T(8,128)(2,1)} %get-tuple-element.111), channel_id=1, source_target_pairs={{0,16},{8,24},{16,0},{24,8},{1,17},{9,25},{17,1},{25,9},{2,18},{10... | collective-permute-start | bytes 442376 | tf_op jit(solution)/shard_map/ppermute | solution.py:33
  323.2 16.1 %collective-permute-start.71 = (bf16[4,24,768]{2,1,0:T(8,128)(2,1)}, bf16[4,24,768]{2,1,0:T(8,128)(2,1)}, u32[]{:S(2)}, u32[]{:S(2)}) collective-permute-start(bf16[4,24,768]{2,1,0:T(8,128)(2,1)} %get-tuple-element.110), channel_id=1, source_target_pairs={{0,8},{8,0},{16,24},{24,16},{1,9},{9,1},{17,25},{25,17},{2,10},{10... | collective-permute-start | bytes 442376 | tf_op jit(solution)/shard_map/ppermute | solution.py:33
  328.3 14.8 %collective-permute-start.83 = (bf16[96,768]{1,0:T(8,128)(2,1)S(1)}, bf16[96,768]{1,0:T(8,128)(2,1)S(1)}, u32[]{:S(2)}, u32[]{:S(2)}) collective-permute-start(bf16[96,768]{1,0:T(8,128)(2,1)S(1)} %copy-done.44), channel_id=1, source_target_pairs={{0,24},{8,16},{16,8},{24,0},{1,25},{9,17},{17,9},{25,1},{2,26},{10... | collective-permute-start | bytes 442376 | tf_op jit(solution)/shard_map/ppermute | solution.py:33
  352.1 12.7 %collective-permute-start.43 = (bf16[2,256,768]{2,1,0:T(8,128)(2,1)S(1)}, bf16[2,256,768]{2,1,0:T(8,128)(2,1)S(1)}, u32[]{:S(2)}, u32[]{:S(2)}) collective-permute-start(bf16[2,256,768]{2,1,0:T(8,128)(2,1)S(1)} %copy-done.53), channel_id=1, source_target_pairs={{0,1},{1,0},{2,3},{3,2},{4,5},{5,4},{6,7},{7,6},{8,9},{9,8},{10,11... | collective-permute-start | bytes 2359304 | tf_op jit(solution)/shard_map/ppermute | solution.py:33
  353.2 13.5 %collective-permute-start.84 = (bf16[96,768]{1,0:T(8,128)(2,1)S(1)}, bf16[96,768]{1,0:T(8,128)(2,1)S(1)}, u32[]{:S(2)}, u32[]{:S(2)}) collective-permute-start(bf16[96,768]{1,0:T(8,128)(2,1)S(1)} %fusion.59), channel_id=1, source_target_pairs={{0,24},{8,16},{16,8},{24,0},{1,25},{9,17},{17,9},{25,1},{2,26},{10... | collective-permute-start | bytes 442376 | tf_op jit(solution)/shard_map/ppermute | solution.py:33
  359.3 16.2 %collective-permute-start.86 = (bf16[96,768]{1,0:T(8,128)(2,1)S(1)}, bf16[96,768]{1,0:T(8,128)(2,1)S(1)}, u32[]{:S(2)}, u32[]{:S(2)}) collective-permute-start(bf16[96,768]{1,0:T(8,128)(2,1)S(1)} %fusion.59), channel_id=1, source_target_pairs={{0,8},{8,0},{16,24},{24,16},{1,9},{9,1},{17,25},{25,17},{2,10},{10... | collective-permute-start | bytes 442376 | tf_op jit(solution)/shard_map/ppermute | solution.py:33
  361.8 14.9 %collective-permute-start.77 = (bf16[24,4,768]{2,0,1:T(8,128)(2,1)S(1)}, bf16[24,4,768]{2,0,1:T(8,128)(2,1)S(1)}, u32[]{:S(2)}, u32[]{:S(2)}) collective-permute-start(bf16[24,4,768]{2,0,1:T(8,128)(2,1)S(1)} %pad_maximum_fusion.9), channel_id=1, source_target_pairs={{0,24},{8,16},{16,8},{24,0},{1,25},{9,17},{17,9},{25,1},{2,26},{10... | collective-permute-start | bytes 442376 | tf_op jit(solution)/shard_map/ppermute | solution.py:33
  364.8 15.4 %collective-permute-start.78 = (bf16[24,4,768]{2,0,1:T(8,128)(2,1)S(1)}, bf16[24,4,768]{2,0,1:T(8,128)(2,1)S(1)}, u32[]{:S(2)}, u32[]{:S(2)}) collective-permute-start(bf16[24,4,768]{2,0,1:T(8,128)(2,1)S(1)} %pad_maximum_fusion.9), channel_id=1, source_target_pairs={{0,16},{8,24},{16,0},{24,8},{1,17},{9,25},{17,1},{25,9},{2,18},{10... | collective-permute-start | bytes 442376 | tf_op jit(solution)/shard_map/ppermute | solution.py:33
  366.7 15.3 %collective-permute-start.79 = (bf16[24,4,768]{2,0,1:T(8,128)(2,1)S(1)}, bf16[24,4,768]{2,0,1:T(8,128)(2,1)S(1)}, u32[]{:S(2)}, u32[]{:S(2)}) collective-permute-start(bf16[24,4,768]{2,0,1:T(8,128)(2,1)S(1)} %pad_maximum_fusion.9), channel_id=1, source_target_pairs={{0,8},{8,0},{16,24},{24,16},{1,9},{9,1},{17,25},{25,17},{2,10},{10... | collective-permute-start | bytes 442376 | tf_op jit(solution)/shard_map/ppermute | solution.py:33
  368.2 61.9 %collective-permute-start.24 = (bf16[256,768]{1,0:T(8,128)(2,1)}, bf16[256,768]{1,0:T(8,128)(2,1)}, u32[]{:S(2)}, u32[]{:S(2)}) collective-permute-start(bf16[256,768]{1,0:T(8,128)(2,1)} %fusion.45), channel_id=1, source_target_pairs={{0,2},{1,3},{2,0},{3,1},{4,6},{5,7},{6,4},{7,5},{8,10},{9,11},{10,... | collective-permute-start | bytes 1179656 | tf_op jit(solution)/shard_map/ppermute | solution.py:33
  375.5 54.7 %collective-permute-start.32 = (bf16[256,768]{1,0:T(8,128)(2,1)}, bf16[256,768]{1,0:T(8,128)(2,1)}, u32[]{:S(2)}, u32[]{:S(2)}) collective-permute-start(bf16[256,768]{1,0:T(8,128)(2,1)} %fusion.46), channel_id=1, source_target_pairs={{0,2},{1,3},{2,0},{3,1},{4,6},{5,7},{6,4},{7,5},{8,10},{9,11},{10,... | collective-permute-start | bytes 1179656 | tf_op jit(solution)/shard_map/ppermute | solution.py:33
  376.7 53.5 %collective-permute-start.40 = (bf16[256,768]{1,0:T(8,128)(2,1)}, bf16[256,768]{1,0:T(8,128)(2,1)}, u32[]{:S(2)}, u32[]{:S(2)}) collective-permute-start(bf16[256,768]{1,0:T(8,128)(2,1)} %fusion.47), channel_id=1, source_target_pairs={{0,2},{1,3},{2,0},{3,1},{4,6},{5,7},{6,4},{7,5},{8,10},{9,11},{10,... | collective-permute-start | bytes 1179656 | tf_op jit(solution)/shard_map/ppermute | solution.py:33
  380.3 42.2 %collective-permute-start.42 = (bf16[256,768]{1,0:T(8,128)(2,1)}, bf16[256,768]{1,0:T(8,128)(2,1)S(1)}, u32[]{:S(2)}, u32[]{:S(2)}) collective-permute-start(bf16[256,768]{1,0:T(8,128)(2,1)} %fusion.48), channel_id=1, source_target_pairs={{0,2},{1,3},{2,0},{3,1},{4,6},{5,7},{6,4},{7,5},{8,10},{9,11},{10,... | collective-permute-start | bytes 1179656 | tf_op jit(solution)/shard_map/ppermute | solution.py:33
  382.0 36.7 %collective-permute-start.46 = (bf16[256,768]{1,0:T(8,128)(2,1)}, bf16[256,768]{1,0:T(8,128)(2,1)}, u32[]{:S(2)}, u32[]{:S(2)}) collective-permute-start(bf16[256,768]{1,0:T(8,128)(2,1)} %fusion.50), channel_id=1, source_target_pairs={{0,2},{1,3},{2,0},{3,1},{4,6},{5,7},{6,4},{7,5},{8,10},{9,11},{10,... | collective-permute-start | bytes 1179656 | tf_op jit(solution)/shard_map/ppermute | solution.py:33
  (100 other events, 817.0 us)
